TPU v7x, 128 devices: a whole 4x4x4 slice. The times are simulated.
128 devices in a mesh: dp: 8 (over x, core), tensor: 16 (over y, z).
Axes of the slice: x: 4, y: 4, z: 4, core: 2. Of those that a mesh axis runs over, the one named last changes fastest.
Arguments:
- tokens: bfloat16 [2048, 4096], P('dp', 'tensor'), may hold values from -6 to 6
- grad_out: bfloat16 [2048, 4096], P('dp', 'tensor'), may hold values from -6 to 6
- w_gate: bfloat16 [4096, 14336], P(None, 'tensor'), may hold values from -0.09375 to 0.09375
- w_up: bfloat16 [4096, 14336], P(None, 'tensor'), may hold values from -0.09375 to 0.09375
- w_down: bfloat16 [14336, 4096], P('tensor'), may hold values from -0.046875 to 0.046875
- active_ids: int32 [8, 56], P('dp'), may hold values from 0 to 111, as said below
- active_count: int32 [8], P('dp'), may hold values from 14 to 56
Outputs:
- input_grad: bfloat16 [2048, 4096], P('dp', 'tensor')
- grad_gate: bfloat16 [4096, 14336], P('dp', 'tensor')
- grad_up: bfloat16 [4096, 14336], P('dp', 'tensor')
- grad_down: bfloat16 [14336, 4096], P('tensor', 'dp')
Inputs may be any that keep to these rules, and one draw needn't show every extreme that they name: `active_ids`: each row lists 56 distinct block numbers; only the first active_count entries of a row are active.
All inputs are finite; a program needn't handle non-finite values.
Results may differ from a plain program's by a relative error of at most 0.019.
Values may be sent and summed in bfloat16 or wider, within the bound.
No kernel may reach another device: no remote copies, remote signals or barrier semaphores. Data moves between devices by JAX's collectives and lax.ppermute only.
A program may use at most 192 MiB of HBM per device.

v0:
```python
import jax
import jax.numpy as jnp
from jax import lax
from jax.sharding import PartitionSpec as P

BLOCK = 128
TILE = 256


def contract_rows(left, right):
    return lax.dot_general(
        left, right, (((0,), (0,)), ((), ())), preferred_element_type=jnp.float32
    )


def contract_cols(left, right):
    return lax.dot_general(
        left, right, (((1,), (1,)), ((), ())), preferred_element_type=jnp.float32
    )


def per_device(tokens, grad_out, w_gate, w_up, w_down, active_ids, active_count):
    x_full, dy_full = (
        lax.all_gather(tokens, "tensor", axis=1, tiled=True),
        lax.all_gather(grad_out, "tensor", axis=1, tiled=True),
    )
    tok_rows = x_full.shape[0]
    f_local = w_gate.shape[1]
    nblk_local = f_local // BLOCK
    tile_count = tok_rows // TILE
    owner = lax.axis_index("tensor")
    block_ids = owner * nblk_local + jnp.arange(nblk_local, dtype=jnp.int32)
    in_range = jnp.arange(active_ids.shape[1], dtype=jnp.int32)[None, :] < active_count[:, None]
    matches = (active_ids[:, :, None] == block_ids[None, None, :]) & in_range[:, :, None]
    tile_mask = jnp.any(matches, axis=1).astype(jnp.float32)
    row_mask = jnp.broadcast_to(
        tile_mask[:, None, :, None], (tile_count, TILE, nblk_local, BLOCK)
    ).reshape(tok_rows, f_local)
    gate = jnp.dot(x_full, w_gate, preferred_element_type=jnp.float32)
    up = jnp.dot(x_full, w_up, preferred_element_type=jnp.float32)
    logistic = jax.nn.sigmoid(gate)
    swish = gate * logistic
    hidden = (swish * up * row_mask).astype(jnp.bfloat16)
    hidden_grad = contract_cols(dy_full, w_down)
    d_gate = (hidden_grad * up * logistic * (1.0 + gate * (1.0 - logistic)) * row_mask).astype(
        jnp.bfloat16
    )
    d_up = (hidden_grad * swish * row_mask).astype(jnp.bfloat16)
    partial_dx = contract_cols(d_gate, w_gate) + contract_cols(d_up, w_up)
    input_grad = lax.psum_scatter(
        partial_dx.astype(jnp.bfloat16), "tensor", scatter_dimension=1, tiled=True
    )
    summed = lax.psum_scatter(
        jnp.concatenate(
            [
                contract_rows(x_full, d_gate),
                contract_rows(x_full, d_up),
                contract_rows(dy_full, hidden),
            ],
            axis=1,
        ).astype(jnp.bfloat16),
        "dp",
        scatter_dimension=0,
        tiled=True,
    ).astype(jnp.float32)
    grad_gate = summed[:, :f_local].astype(jnp.bfloat16)
    grad_up = summed[:, f_local : 2 * f_local].astype(jnp.bfloat16)
    grad_down = summed[:, 2 * f_local :].T.astype(jnp.bfloat16)
    return (input_grad, grad_gate, grad_up, grad_down)


def solution(mesh):
    in_specs = (
        P("dp", "tensor"),
        P("dp", "tensor"),
        P(None, "tensor"),
        P(None, "tensor"),
        P("tensor", None),
        P("dp", None),
        P("dp"),
    )
    out_specs = (P("dp", "tensor"), P("dp", "tensor"), P("dp", "tensor"), P("tensor", "dp"))
    return jax.shard_map(
        per_device, mesh=mesh, in_specs=in_specs, out_specs=out_specs, check_vma=False
    )
```

profile of v0, /device:TPU:1, one launch (start us, length us, event | category | flops | bytes accessed | tf_op | source)
XLA Modules:
  0.0 349.4 jit_solution(9819686625621746978)
XLA Ops:
  7.2 0.7 all-gather.5.cloned.1.call-update
  7.9 0.0 all-gather.3.cloned.1.call-start
  7.9 0.7 all-gather.3.cloned.1.call-update
  8.6 0.0 reduce-scatter.5.cloned.1.call-start
  9.4 0.8 and_reduce_fusion
  10.2 0.1 broadcast_bitcast_fusion
  10.3 50.0 %all-gather.5.cloned.1.call-done = bf16[256,4096]{1,0:T(8,128)(2,1)} async-done(((bf16[256,256]{1,0:T(8,128)(2,1)}), bf16[256,4096]{1,0:T(8,128)(2,1)}) %all-gather.5.cloned.1.call-update) | async-done | bytes 2097168 | tf_op jit(solution)/shard_map/all_gather | solution.py:24
  60.3 6.2 %fusion.6 = f32[256,896]{1,0:T(8,128)S(1)} fusion(bf16[256,4096]{1,0:T(8,128)(2,1)} %all-gather.5.cloned.1.call-done, bf16[4096,896]{1,0:T(8,128)(2,1)} %param.9), kind=kOutput, calls=%fused_computation.19 | convolution fusion | flops 1879048192 | bytes 10354688 | tf_op jit(solution)/shard_map/dot_general | solution.py:39
  66.5 6.3 %fusion.5 = f32[256,896]{1,0:T(8,128)} fusion(bf16[256,4096]{1,0:T(8,128)(2,1)S(1)} %copy-done, bf16[4096,896]{1,0:T(8,128)(2,1)} %param.10), kind=kOutput, calls=%fused_computation.18 | convolution fusion | flops 1879048192 | bytes 10354688 | tf_op jit(solution)/shard_map/dot_general | solution.py:40
  72.9 36.6 %all-gather.3.cloned.1.call-done = bf16[256,4096]{1,0:T(8,128)(2,1)} async-done(((bf16[256,256]{1,0:T(8,128)(2,1)}), bf16[256,4096]{1,0:T(8,128)(2,1)}) %all-gather.3.cloned.1.call-update) | async-done | bytes 2097168 | tf_op jit(solution)/shard_map/all_gather | solution.py:25
  109.5 7.2 %convert_bitcast_fusion = bf16[4096,896]{0,1:T(8,128)(2,1)} fusion(bf16[256,4096]{1,0:T(8,128)(2,1)} %all-gather.3.cloned.1.call-done, f32[256,896]{1,0:T(8,128)} %fusion.5, f32[896]{0:T(1024)S(1)} %broadcast_bitcast_fusion, f32[256,896]{1,0:T(8,128)S(1)} %fusion.6), kind=kOutput, calls=%fused_computation.1 | convolution fusion | flops 1884323840 | bytes 11275776 | tf_op jit(solution)/shard_map/dot_general | solution.py:11
  116.7 2.7 multiply_convert_fusion.1
  119.4 5.1 %convert_bitcast_fusion.1 = bf16[4096,896]{0,1:T(8,128)(2,1)} fusion(bf16[256,896]{1,0:T(8,128)(2,1)S(1)} %get-tuple-element.15, bf16[256,4096]{1,0:T(8,128)(2,1)S(1)} %copy-done), kind=kOutput, calls=%fused_computation.2 | convolution fusion | flops 1882718208 | bytes 9895936 | tf_op jit(solution)/shard_map/dot_general | solution.py:11
  124.4 5.3 %convert_bitcast_fusion.2 = bf16[4096,896]{0,1:T(8,128)(2,1)} fusion(bf16[256,896]{1,0:T(8,128)(2,1)S(1)} %get-tuple-element.16, bf16[256,4096]{1,0:T(8,128)(2,1)S(1)} %copy-done), kind=kOutput, calls=%fused_computation.3 | convolution fusion | flops 1882718208 | bytes 9895936 | tf_op jit(solution)/shard_map/dot_general | solution.py:11
  129.8 20.1 %pad_maximum_fusion = bf16[4096,2688]{0,1:T(8,128)(2,1)} fusion(bf16[4096,896]{0,1:T(8,128)(2,1)} %convert_bitcast_fusion, bf16[4096,896]{0,1:T(8,128)(2,1)} %convert_bitcast_fusion.1, bf16[4096,896]{0,1:T(8,128)(2,1)} %convert_bitcast_fusion.2), kind=kLoop, calls=%fused_computation | loop fusion | flops 66060288 | bytes 44040192 | tf_op jit(solution)/shard_map/concatenate | solution.py:54
  149.9 0.0 reduce-scatter.3.cloned.1.call-start
  150.0 0.9 copy-done.4
  150.9 5.4 %fusion.7 = f32[256,4096]{1,0:T(8,128)S(1)} fusion(bf16[256,896]{1,0:T(8,128)(2,1)S(1)} %copy-done.4, bf16[4096,896]{1,0:T(8,128)(2,1)} %param.9), kind=kOutput, calls=%fused_computation.20 | convolution fusion | flops 1879048192 | bytes 11993088 | tf_op jit(solution)/shard_map/dot_general | solution.py:17
  156.3 7.3 %fusion = bf16[256,4096]{1,0:T(8,128)(2,1)} fusion(f32[256,4096]{1,0:T(8,128)S(1)} %fusion.7, bf16[256,896]{1,0:T(8,128)(2,1)S(1)} %get-tuple-element.15, bf16[4096,896]{1,0:T(8,128)(2,1)} %param.10), kind=kOutput, calls=%fused_computation.5 | convolution fusion | flops 1881145344 | bytes 14090240 | tf_op jit(solution)/shard_map/dot_general | solution.py:17
  163.7 102.4 %reduce-scatter.5.cloned.1.call-done = bf16[512,2688]{0,1:T(8,128)(2,1)} async-done(((bf16[4096,2688]{0,1:T(8,128)(2,1)}), bf16[512,2688]{0,1:T(8,128)(2,1)}) %reduce-scatter.5.cloned.1.call-update) | async-done | bytes 2752528 | tf_op jit(solution)/shard_map/reduce_scatter | solution.py:53
  266.1 2.8 slice_bitcast_fusion
  268.9 1.3 copy.14
  270.2 1.3 copy.13
  271.4 71.4 %reduce-scatter.3.cloned.1.call-done = bf16[256,256]{1,0:T(8,128)(2,1)} async-done(((bf16[256,4096]{1,0:T(8,128)(2,1)}), bf16[256,256]{1,0:T(8,128)(2,1)}) %reduce-scatter.3.cloned.1.call-update) | async-done | bytes 131088 | tf_op jit(solution)/shard_map/reduce_scatter | solution.py:50
  (17 shorter events, 0.1 us)
Async XLA Ops:
  7.2 53.1 %all-gather.5.cloned.1.call-start = ((), (), s32[]{:S(2)}) async-start(), calls=%async_computation.3 | async-start | bytes 2228224 | tf_op jit(solution)/shard_map/all_gather | solution.py:24
  7.9 101.6 %all-gather.3.cloned.1.call-start = ((), (), s32[]{:S(2)}) async-start(), calls=%async_computation.2 | async-start | bytes 2228224 | tf_op jit(solution)/shard_map/all_gather | solution.py:25
  8.6 257.4 %reduce-scatter.5.cloned.1.call-start = ((), (), s32[]{:S(2)}) async-start(), calls=%async_computation.5 | async-start | bytes 24772608 | tf_op jit(solution)/shard_map/reduce_scatter | solution.py:53
  60.3 6.2 %copy-start = (bf16[256,4096]{1,0:T(8,128)(2,1)S(1)}, bf16[256,4096]{1,0:T(8,128)(2,1)}, u32[]{:S(2)}) copy-start(bf16[256,4096]{1,0:T(8,128)(2,1)} %all-gather.5.cloned.1.call-done) | copy-start | bytes 6291460
  109.5 7.2 %copy-start.1 = (bf16[256,4096]{1,0:T(8,128)(2,1)S(1)}, bf16[256,4096]{1,0:T(8,128)(2,1)}, u32[]{:S(2)}) copy-start(bf16[256,4096]{1,0:T(8,128)(2,1)} %all-gather.3.cloned.1.call-done) | copy-start | bytes 6291460
  109.5 7.2 %copy-start.2 = (f32[256,896]{1,0:T(8,128)S(1)}, f32[256,896]{1,0:T(8,128)}, u32[]{:S(2)}) copy-start(f32[256,896]{1,0:T(8,128)} %fusion.5) | copy-start | bytes 2752516
  109.5 7.2 %copy-start.5 = (bf16[896,4096]{1,0:T(8,128)(2,1)S(1)}, bf16[896,4096]{1,0:T(8,128)(2,1)}, u32[]{:S(2)}) copy-start(bf16[896,4096]{1,0:T(8,128)(2,1)} %param.11) | copy-start | bytes 22020100
  119.3 5.1 %copy-start.3 = (bf16[256,896]{1,0:T(8,128)(2,1)}, bf16[256,896]{1,0:T(8,128)(2,1)S(1)}, u32[]{:S(2)}) copy-start(bf16[256,896]{1,0:T(8,128)(2,1)S(1)} %get-tuple-element.16) | copy-start | bytes 1376260
  149.9 1.0 copy-start.4
  149.9 193.0 %reduce-scatter.3.cloned.1.call-start = ((), (), s32[]{:S(2)}) async-start(), calls=%async_computation.4 | async-start | bytes 2228224 | tf_op jit(solution)/shard_map/reduce_scatter | solution.py:50
Sparse Core Ops, SparseCore 0:
  10.1 50.1 all-gather.4
  62.4 47.0 all-gather.2
  150.0 115.9 reduce-scatter.4
  269.8 73.0 reduce-scatter.2
where the time goes:
time: 351 us; the launch traced here: 349 us
  waiting for transfers between devices  262 us (75%)
  matrix products  45.5 us (13%)
  other arithmetic  21 us (6%)
  between operations  14.5 us (4%)
  local copies, waits for them, and re-layouts  6.4 us (2%)
    reduce_scatter x1, waiting for transfers between devices, per_device(): lax.psum_scatter(jnp.concatenate([contract_rows(x_full, d_gate), contract...  102 us
    reduce_scatter x1, waiting for transfers between devices, per_device(): lax.psum_scatter(partial_dx.astype(jnp.bfloat16), 'tensor', scatter_dimen...  71.4 us
    all_gather x1, waiting for transfers between devices, per_device(): lax.all_gather(tokens, 'tensor', axis=1, tiled=True)  50 us
    all_gather x1, waiting for transfers between devices, per_device(): lax.all_gather(grad_out, 'tensor', axis=1, tiled=True)  36.6 us
    concatenate x1, other arithmetic, per_device(): jnp.concatenate([contract_rows(x_full, d_gate), contract_rows(x_full, d_u...  20.1 us
    dot_general x3, matrix products, contract_rows(): lax.dot_general(left, right, (((0,), (0,)), ((), ())), preferred_element_...  17.6 us
    dot_general x3, matrix products, contract_cols(): lax.dot_general(left, right, (((1,), (1,)), ((), ())), preferred_element_...  15.4 us
  transfers between devices with their start and end apart: 4, of which 4 were waited for; matrix products, arithmetic and copies ran while one was open for 9% of the time, Pallas kernels for 0%

commit v1 on v0

v1 whole, which is shorter than its diff:
```python
import jax
import jax.numpy as jnp
from jax import lax
from jax.experimental import pallas as pl
from jax.experimental.pallas import tpu as pltpu
from jax.sharding import Mesh, PartitionSpec as P

BLOCK = 128
RING = 4
OFFSETS = (0, 1, 3, 2)


def from_offset(value, axis, offset):
    return lax.ppermute(value, axis, [(i, (i - offset) % RING) for i in range(RING)])


def gather_ring(stack, axis):
    half = stack.shape[1] // 2
    after = from_offset(stack, axis, 1)
    before = from_offset(stack, axis, 3)
    low = from_offset(after[:, :half], axis, 1)
    high = from_offset(before[:, half:], axis, 3)
    return jnp.concatenate([stack, after, before, jnp.concatenate([low, high], axis=1)], axis=0)


def forward_kernel(jt, jg, active, x, dy, wg, wu, wd, out, gate_acc, up_acc, hid_acc):
    step = pl.program_id(0)
    nblk = out.shape[1] // 3 // BLOCK
    f_local = nblk * BLOCK
    gate_part = jnp.dot(x[0], wg[...], preferred_element_type=jnp.float32)
    up_part = jnp.dot(x[0], wu[...], preferred_element_type=jnp.float32)
    hid_part = lax.dot_general(
        dy[0], wd[...], (((1,), (1,)), ((), ())), preferred_element_type=jnp.float32
    )

    @pl.when(step == 0)
    def _():
        gate_acc[...] = gate_part
        up_acc[...] = up_part
        hid_acc[...] = hid_part

    @pl.when(step > 0)
    def _():
        gate_acc[...] += gate_part
        up_acc[...] += up_part
        hid_acc[...] += hid_part

    @pl.when(step == pl.num_programs(0) - 1)
    def _():
        for b in range(nblk):
            cols = pl.ds(b * BLOCK, BLOCK)
            on = active[b] > 0
            gate, up, hid = gate_acc[:, cols], up_acc[:, cols], hid_acc[:, cols]
            logistic = jax.nn.sigmoid(gate)
            swish = gate * logistic
            hidden = swish * up
            d_gate = hid * up * logistic * (1.0 + gate * (1.0 - logistic))
            d_up = hid * swish
            for k, value in enumerate((hidden, d_gate, d_up)):
                out[:, pl.ds(k * f_local + b * BLOCK, BLOCK)] = jnp.where(on, value, 0.0).astype(
                    out.dtype
                )


def forward(jt, jg, active, x, dy, wg, wu, wd):
    n, rows, depth = x.shape
    f_local = wg.shape[1]
    return pl.pallas_call(
        forward_kernel,
        grid_spec=pltpu.PrefetchScalarGridSpec(
            num_scalar_prefetch=3,
            grid=(n,),
            in_specs=[
                pl.BlockSpec((1, rows, depth), lambda i, jt, jg, a: (i, 0, 0)),
                pl.BlockSpec((1, rows, depth), lambda i, jt, jg, a: (i, 0, 0)),
                pl.BlockSpec((depth, f_local), lambda i, jt, jg, a: (jt[i], 0)),
                pl.BlockSpec((depth, f_local), lambda i, jt, jg, a: (jt[i], 0)),
                pl.BlockSpec((f_local, depth), lambda i, jt, jg, a: (0, jg[i])),
            ],
            out_specs=pl.BlockSpec((rows, 3 * f_local), lambda i, jt, jg, a: (0, 0)),
            scratch_shapes=[pltpu.VMEM((rows, f_local), jnp.float32)] * 3,
        ),
        out_shape=jax.ShapeDtypeStruct((rows, 3 * f_local), jnp.bfloat16),
        compiler_params=pltpu.CompilerParams(vmem_limit_bytes=40 * 2**20),
        cost_estimate=pl.CostEstimate(
            flops=6 * n * rows * depth * f_local,
            bytes_accessed=6 * n * depth * f_local + 4 * n * rows * depth,
            transcendentals=rows * f_local,
        ),
        name="forward",
    )(jt, jg, active, x, dy, wg, wu, wd)


def backward_kernel(js, act, wg, wu, out):
    f_local = wg.shape[1]
    rows_t = (((1,), (1,)), ((), ()))
    total = lax.dot_general(
        act[:, pl.ds(f_local, f_local)], wg[...], rows_t, preferred_element_type=jnp.float32
    )
    total += lax.dot_general(
        act[:, pl.ds(2 * f_local, f_local)], wu[...], rows_t, preferred_element_type=jnp.float32
    )
    out[0] = total.astype(out.dtype)


def backward(js, act, wg, wu):
    n = js.shape[0]
    rows = act.shape[0]
    d_model, f_local = wg.shape
    depth = d_model // n
    return pl.pallas_call(
        backward_kernel,
        grid_spec=pltpu.PrefetchScalarGridSpec(
            num_scalar_prefetch=1,
            grid=(n,),
            in_specs=[
                pl.BlockSpec((rows, 3 * f_local), lambda i, js: (0, 0)),
                pl.BlockSpec((depth, f_local), lambda i, js: (js[i], 0)),
                pl.BlockSpec((depth, f_local), lambda i, js: (js[i], 0)),
            ],
            out_specs=pl.BlockSpec((1, rows, depth), lambda i, js: (i, 0, 0)),
        ),
        out_shape=jax.ShapeDtypeStruct((n, rows, depth), jnp.bfloat16),
        compiler_params=pltpu.CompilerParams(vmem_limit_bytes=40 * 2**20),
        cost_estimate=pl.CostEstimate(
            flops=4 * rows * d_model * f_local,
            bytes_accessed=4 * d_model * f_local + 2 * rows * d_model,
            transcendentals=0,
        ),
        name="backward",
    )(js, act, wg, wu)


def weights_kernel(index, *refs):
    acts, pieces = refs[:10], refs[10]
    out_gate, out_up, out_down = refs[11:14]
    act_buf, piece_buf, gate_acc, up_acc, down_acc, act_sem, piece_sem = refs[14:]
    tiles, rows, wide = act_buf.shape
    f_local = wide // 3
    depth = piece_buf.shape[2]
    half = rows // 2
    copies = []
    for t in range(tiles):
        mine = []
        if t % 4 == 3:
            parts = [(acts[t // 4 * 5 + 3], 0, half), (acts[t // 4 * 5 + 4], half, half)]
        else:
            parts = [(acts[t // 4 * 5 + t % 4], 0, rows)]
        for p, (ref, start, size) in enumerate(parts):
            mine.append(
                pltpu.make_async_copy(ref, act_buf.at[t, pl.ds(start, size)], act_sem.at[t, p])
            )
        for h in range(2):
            mine.append(
                pltpu.make_async_copy(
                    pieces.at[index[t, h]], piece_buf.at[2 * t + h], piece_sem.at[t, h]
                )
            )
        copies.append(mine)
    for mine in copies:
        for copy in mine:
            copy.start()
    first_t = (((0,), (0,)), ((), ()))
    for t in range(tiles):
        for copy in copies[t]:
            copy.wait()
        for h in range(2):
            tok = piece_buf[2 * t + h, pl.ds(0, rows), :]
            cot = piece_buf[2 * t + h, pl.ds(rows, rows), :]
            cols = pl.ds(h * depth, depth)
            g = lax.dot_general(
                tok, act_buf[t, :, pl.ds(f_local, f_local)], first_t,
                preferred_element_type=jnp.float32,
            )
            u = lax.dot_general(
                tok, act_buf[t, :, pl.ds(2 * f_local, f_local)], first_t,
                preferred_element_type=jnp.float32,
            )
            d = lax.dot_general(
                act_buf[t, :, pl.ds(0, f_local)], cot, first_t,
                preferred_element_type=jnp.float32,
            )
            if t == 0:
                gate_acc[cols, :] = g
                up_acc[cols, :] = u
                down_acc[:, cols] = d
            elif t < tiles - 1:
                gate_acc[cols, :] += g
                up_acc[cols, :] += u
                down_acc[:, cols] += d
            else:
                out_gate[cols, :] = (gate_acc[cols, :] + g).astype(out_gate.dtype)
                out_up[cols, :] = (up_acc[cols, :] + u).astype(out_up.dtype)
                out_down[:, cols] = (down_acc[:, cols] + d).astype(out_down.dtype)


def weight_grads(index, acts, pieces):
    tiles = index.shape[0]
    rows, wide = acts[0].shape
    f_local = wide // 3
    depth = pieces.shape[2]
    anywhere = pl.BlockSpec(memory_space=pl.ANY)
    whole = pl.BlockSpec(memory_space=pltpu.VMEM)
    return pl.pallas_call(
        weights_kernel,
        in_specs=[pl.BlockSpec(memory_space=pltpu.SMEM)] + [anywhere] * 11,
        out_specs=[whole] * 3,
        out_shape=[
            jax.ShapeDtypeStruct((2 * depth, f_local), jnp.bfloat16),
            jax.ShapeDtypeStruct((2 * depth, f_local), jnp.bfloat16),
            jax.ShapeDtypeStruct((f_local, 2 * depth), jnp.bfloat16),
        ],
        scratch_shapes=[
            pltpu.VMEM((tiles, rows, wide), jnp.bfloat16),
            pltpu.VMEM((2 * tiles, 2 * rows, depth), jnp.bfloat16),
            pltpu.VMEM((2 * depth, f_local), jnp.float32),
            pltpu.VMEM((2 * depth, f_local), jnp.float32),
            pltpu.VMEM((f_local, 2 * depth), jnp.float32),
            pltpu.SemaphoreType.DMA((tiles, 2)),
            pltpu.SemaphoreType.DMA((tiles, 2)),
        ],
        compiler_params=pltpu.CompilerParams(vmem_limit_bytes=48 * 2**20),
        cost_estimate=pl.CostEstimate(
            flops=2 * tiles * rows * 2 * depth * wide,
            bytes_accessed=2 * tiles * rows * wide + 4 * tiles * rows * 2 * depth,
            transcendentals=0,
        ),
        name="weight_grads",
    )(index, *acts, pieces)


def per_device(tokens, grad_out, w_gate, w_up, w_down, active_ids, active_count):
    rows, depth = tokens.shape
    f_local = w_gate.shape[1]
    nblk = f_local // BLOCK
    x, c, y, z = (lax.axis_index(a) for a in ("x", "c", "y", "z"))
    off = jnp.array(OFFSETS, jnp.int32)

    to_columns = [
        (
            ((sx * 2 + sc) * 4 + sy) * 4 + sz,
            ((sy * 2 + sz // 2) * 4 + sx) * 4 + (sz % 2) * 2 + sc,
        )
        for sx in range(4)
        for sc in range(2)
        for sy in range(4)
        for sz in range(4)
    ]
    both = jnp.concatenate([tokens, grad_out], axis=0)
    turned = lax.ppermute(both, ("x", "c", "y", "z"), to_columns)
    pieces = lax.all_gather(turned, ("y", "z"))

    x_rel = gather_ring(gather_ring(tokens[None], "z"), "y")
    dy_rel = gather_ring(gather_ring(grad_out[None], "y"), "z")
    slow, fast = jnp.repeat(off, 4), jnp.tile(off, 4)
    jt = (y + slow) % 4 * 4 + (z + fast) % 4
    jg = (y + fast) % 4 * 4 + (z + slow) % 4

    block_ids = (y * 4 + z) * nblk + jnp.arange(nblk, dtype=jnp.int32)
    listed = jnp.arange(active_ids.shape[1], dtype=jnp.int32) < active_count[0]
    matches = (active_ids[0][:, None] == block_ids[None, :]) & listed[:, None]
    active = jnp.any(matches, axis=0).astype(jnp.int32)

    act = forward(jt, jg, active, x_rel, dy_rel, w_gate, w_up, w_down)

    half = rows // 2
    after = from_offset(act, "x", 1)
    before = from_offset(act, "x", 3)
    low = from_offset(after[:half], "x", 1)
    high = from_offset(before[half:], "x", 3)
    acts = [act, after, before, low, high]
    swapped = [lax.ppermute(a, "c", [(0, 1), (1, 0)]) for a in acts]

    partial_dx = backward(jnp.arange(16, dtype=jnp.int32), act, w_gate, w_up)
    shares = lax.all_to_all(partial_dx, ("y", "z"), 0, 0)
    input_grad = jnp.sum(shares.astype(jnp.float32), axis=0).astype(jnp.bfloat16)

    tile_x = (x + off) % 4
    index = jnp.concatenate(
        [
            tile_x[:, None] * 4 + jnp.array([0, 2], jnp.int32)[None, :] + core
            for core in (c, 1 - c)
        ]
    )
    grads = weight_grads(index.astype(jnp.int32), acts + swapped, pieces)
    return (input_grad, *grads)


def solution(mesh):
    fine = Mesh(mesh.devices.reshape(4, 2, 4, 4), ("x", "c", "y", "z"))
    dp, tensor = ("x", "c"), ("y", "z")
    in_specs = (
        P(dp, tensor),
        P(dp, tensor),
        P(None, tensor),
        P(None, tensor),
        P(tensor, None),
        P(dp, None),
        P(dp),
    )
    out_specs = (P(dp, tensor), P(dp, tensor), P(dp, tensor), P(tensor, dp))
    return jax.shard_map(
        per_device, mesh=fine, in_specs=in_specs, out_specs=out_specs, check_vma=False
    )
```

time: 351 us -> 175 us (0.50)
  waiting for transfers between devices: 262 us -> 40.7 us
  starting transfers between devices: 0.16 us -> 62.8 us
  matrix products: 45.5 us -> 0 us
  Pallas kernels: 0 us -> 45.1 us
  other arithmetic: 21 us -> 5.44 us
    reduce_scatter x2 -> x0, waiting for transfers between devices: 174 us -> none  [the longest x1 102 us: per_device(): lax.psum_scatter(jnp.concatenate([contract_rows(x_full, d_gate), contract...]
    all_gather x2 -> x1, waiting for transfers between devices: 86.7 us -> 0.02 us  [per_device(): pieces = lax.all_gather(turned, ('y', 'z'))]
    ppermute x0 -> x26, starting transfers between devices: none -> 58.3 us  [the longest x20 34.7 us: from_offset(): lax.ppermute(value, axis, [(i, (i - offset) % RING) for i in range(RING)])]
    dot_general x8 -> x0, matrix products: 45.5 us -> none  [the longest x3 17.6 us: contract_rows(): lax.dot_general(left, right, (((0,), (0,)), ((), ())), preferred_element_...]
    pallas_call x0 -> x3, Pallas kernels: none -> 45.1 us  [the longest x1 18.5 us: forward(): pl.pallas_call(forward_kernel, grid_spec=pltpu.PrefetchScalarGridSpec(num...]
    ppermute x0 -> x26, waiting for transfers between devices: none -> 40.7 us  [the longest x20 34.7 us: from_offset(): lax.ppermute(value, axis, [(i, (i - offset) % RING) for i in range(RING)])]
    concatenate x1 -> x6, other arithmetic: 20.1 us -> 1.26 us  [the longest x1 1.04 us: per_device(): both = jnp.concatenate([tokens, grad_out], axis=0)]
    all_to_all x0 -> x1, starting transfers between devices: none -> 4.44 us  [per_device(): shares = lax.all_to_all(partial_dx, ('y', 'z'), 0, 0)]
  transfers between devices with their start and end apart: 4 -> 28, of which waited for: 4 -> 8; matrix products, arithmetic and copies ran while one was open for 9% -> 5% of each run, Pallas kernels for 0% -> 19%
where the time goes in v1:
time: 175 us; the launch traced here: 174 us
  starting transfers between devices  62.8 us (36%)
  Pallas kernels  45.1 us (26%)
  waiting for transfers between devices  40.7 us (23%)
  between operations  15.1 us (9%)
  other arithmetic  5.44 us (3%)
  local copies, waits for them, and re-layouts  4.63 us (3%)
    ppermute x20, starting transfers between devices, from_offset(): lax.ppermute(value, axis, [(i, (i - offset) % RING) for i in range(RING)])  34.7 us
    ppermute x20, waiting for transfers between devices, from_offset(): lax.ppermute(value, axis, [(i, (i - offset) % RING) for i in range(RING)])  34.7 us
    ppermute x5, starting transfers between devices, per_device(): swapped = [lax.ppermute(a, 'c', [(0, 1), (1, 0)]) for a in acts]  18.7 us
    pallas_call x1, Pallas kernels, forward(): pl.pallas_call(forward_kernel, grid_spec=pltpu.PrefetchScalarGridSpec(num...  18.5 us
    pallas_call x1, Pallas kernels, backward(): pl.pallas_call(backward_kernel, grid_spec=pltpu.PrefetchScalarGridSpec(nu...  14.2 us
    pallas_call x1, Pallas kernels, weight_grads(): pl.pallas_call(weights_kernel, in_specs=[pl.BlockSpec(memory_space=pltpu....  12.4 us
    ppermute x1, waiting for transfers between devices, per_device(): turned = lax.ppermute(both, ('x', 'c', 'y', 'z'), to_columns)  6 us
    ppermute x1, starting transfers between devices, per_device(): turned = lax.ppermute(both, ('x', 'c', 'y', 'z'), to_columns)  4.94 us
  transfers between devices with their start and end apart: 28, of which 8 were waited for; matrix products, arithmetic and copies ran while one was open for 5% of the time, Pallas kernels for 19%

profile of v1, /device:TPU:1, one launch (start us, length us, event | category | flops | bytes accessed | tf_op | source)
XLA Modules:
  0.0 173.7 jit_solution(1329192249648736156)
XLA Ops:
  8.3 4.9 %collective-permute-start.25 = (bf16[512,256]{1,0:T(8,128)(2,1)S(1)}, bf16[512,256]{1,0:T(8,128)(2,1)S(1)}, u32[]{:S(2)}, u32[]{:S(2)}) collective-permute-start(bf16[512,256]{1,0:T(8,128)(2,1)S(1)} %pad_maximum_fusion), channel_id=1, source_target_pairs={{0,0},{1,2},{2,16},{3,18},{4,32},{5,34},{6,48},{7,50},{8,64},{9,66... | collective-permute-start | bytes 786440 | tf_op jit(solution)/shard_map/ppermute | solution.py:250
  13.2 6.0 %collective-permute-done.25 = bf16[512,256]{1,0:T(8,128)(2,1)S(1)} collective-permute-done((bf16[512,256]{1,0:T(8,128)(2,1)S(1)}, bf16[512,256]{1,0:T(8,128)(2,1)S(1)}, u32[]{:S(2)}, u32[]{:S(2)}) %collective-permute-start.25) | collective-permute-done | bytes 262176 | tf_op jit(solution)/shard_map/ppermute | solution.py:250
  20.0 14.4 %collective-permute-start.8 = (bf16[1,256,256]{2,1,0:T(8,128)(2,1)}, bf16[1,256,256]{2,1,0:T(8,128)(2,1)S(1)}, u32[]{:S(2)}, u32[]{:S(2)}) collective-permute-start(bf16[1,256,256]{2,1,0:T(8,128)(2,1)} %bitcast.8), channel_id=1, source_target_pairs={{0,12},{4,0},{8,4},{12,8},{1,13},{5,1},{9,5},{13,9},{2,14},{6,2},{... | collective-permute-start | bytes 393224 | tf_op jit(solution)/shard_map/ppermute | solution.py:14
  40.4 2.7 %collective-permute-start.10 = (bf16[1,128,256]{2,1,0:T(8,128)(2,1)S(1)}, bf16[1,128,256]{2,1,0:T(8,128)(2,1)S(1)}, u32[]{:S(2)}, u32[]{:S(2)}) collective-permute-start(bf16[1,128,256]{2,1,0:T(8,128)(2,1)S(1)} %slice.44), channel_id=1, source_target_pairs={{0,12},{4,0},{8,4},{12,8},{1,13},{5,1},{9,5},{13,9},{2,14},{6,2},{... | collective-permute-start | bytes 196616 | tf_op jit(solution)/shard_map/ppermute | solution.py:14
  43.3 2.1 %collective-permute-start.2 = (bf16[1,128,256]{2,1,0:T(8,128)(2,1)S(1)}, bf16[1,128,256]{2,1,0:T(8,128)(2,1)S(1)}, u32[]{:S(2)}, u32[]{:S(2)}) collective-permute-start(bf16[1,128,256]{2,1,0:T(8,128)(2,1)S(1)} %slice.40), channel_id=1, source_target_pairs={{0,3},{1,0},{2,1},{3,2},{4,7},{5,4},{6,5},{7,6},{8,11},{9,8},{10,9... | collective-permute-start | bytes 196616 | tf_op jit(solution)/shard_map/ppermute | solution.py:14
  45.6 2.1 %collective-permute-done.11 = bf16[1,128,256]{2,1,0:T(8,128)(2,1)S(1)} collective-permute-done((bf16[1,128,256]{2,1,0:T(8,128)(2,1)S(1)}, bf16[1,128,256]{2,1,0:T(8,128)(2,1)S(1)}, u32[]{:S(2)}, u32[]{:S(2)}) %collective-permute-start.11) | collective-permute-done | bytes 65568 | tf_op jit(solution)/shard_map/ppermute | solution.py:14
  47.7 2.3 %collective-permute-start.12 = (bf16[4,256,256]{2,1,0:T(8,128)(2,1)S(1)}, bf16[4,256,256]{2,1,0:T(8,128)(2,1)S(1)}, u32[]{:S(2)}, u32[]{:S(2)}) collective-permute-start(bf16[4,256,256]{2,1,0:T(8,128)(2,1)S(1)} %maximum_maximum_fusion.1), channel_id=1, source_target_pairs={{0,3},{1,0},{2,1},{3,2},{4,7},{5,4},{6,5},{7,6},{8,11},{9,8},{10,9... | collective-permute-start | bytes 1572872 | tf_op jit(solution)/shard_map/ppermute | solution.py:14
  50.2 2.9 %collective-permute-start.4 = (bf16[4,256,256]{2,1,0:T(8,128)(2,1)S(1)}, bf16[4,256,256]{2,1,0:T(8,128)(2,1)S(1)}, u32[]{:S(2)}, u32[]{:S(2)}) collective-permute-start(bf16[4,256,256]{2,1,0:T(8,128)(2,1)S(1)} %maximum_maximum_fusion), channel_id=1, source_target_pairs={{0,12},{4,0},{8,4},{12,8},{1,13},{5,1},{9,5},{13,9},{2,14},{6,2},{... | collective-permute-start | bytes 1572872 | tf_op jit(solution)/shard_map/ppermute | solution.py:14
  53.2 7.1 %collective-permute-done.12 = bf16[4,256,256]{2,1,0:T(8,128)(2,1)S(1)} collective-permute-done((bf16[4,256,256]{2,1,0:T(8,128)(2,1)S(1)}, bf16[4,256,256]{2,1,0:T(8,128)(2,1)S(1)}, u32[]{:S(2)}, u32[]{:S(2)}) %collective-permute-start.12) | collective-permute-done | bytes 524320 | tf_op jit(solution)/shard_map/ppermute | solution.py:14
  60.4 2.6 %collective-permute-start.14 = (bf16[4,128,256]{2,1,0:T(8,128)(2,1)S(1)}, bf16[4,128,256]{2,1,0:T(8,128)(2,1)S(1)}, u32[]{:S(2)}, u32[]{:S(2)}) collective-permute-start(bf16[4,128,256]{2,1,0:T(8,128)(2,1)S(1)} %slice.46), channel_id=1, source_target_pairs={{0,3},{1,0},{2,1},{3,2},{4,7},{5,4},{6,5},{7,6},{8,11},{9,8},{10,9... | collective-permute-start | bytes 786440 | tf_op jit(solution)/shard_map/ppermute | solution.py:14
  63.1 1.2 collective-permute-start.6
  65.0 7.4 %collective-permute-done.14 = bf16[4,128,256]{2,1,0:T(8,128)(2,1)S(1)} collective-permute-done((bf16[4,128,256]{2,1,0:T(8,128)(2,1)S(1)}, bf16[4,128,256]{2,1,0:T(8,128)(2,1)S(1)}, u32[]{:S(2)}, u32[]{:S(2)}) %collective-permute-start.14) | collective-permute-done | bytes 262176 | tf_op jit(solution)/shard_map/ppermute | solution.py:14
  72.3 2.5 %collective-permute-done.15 = bf16[4,128,256]{2,1,0:T(8,128)(2,1)S(1)} collective-permute-done((bf16[4,128,256]{2,1,0:T(8,128)(2,1)S(1)}, bf16[4,128,256]{2,1,0:T(8,128)(2,1)S(1)}, u32[]{:S(2)}, u32[]{:S(2)}) %collective-permute-start.15) | collective-permute-done | bytes 262176 | tf_op jit(solution)/shard_map/ppermute | solution.py:14
  74.8 3.9 %collective-permute-done.7 = bf16[4,128,256]{2,1,0:T(8,128)(2,1)S(1)} collective-permute-done((bf16[4,128,256]{2,1,0:T(8,128)(2,1)S(1)}, bf16[4,128,256]{2,1,0:T(8,128)(2,1)S(1)}, u32[]{:S(2)}, u32[]{:S(2)}) %collective-permute-start.7) | collective-permute-done | bytes 262176 | tf_op jit(solution)/shard_map/ppermute | solution.py:14
  78.8 18.5 %forward.1.act.refs_0_ = bf16[256,2688]{1,0:T(8,128)(2,1)S(1)} custom-call(s32[16]{0:T(128)S(1)} %get-tuple-element.15.jt, s32[16]{0:T(128)S(1)} %get-tuple-element.16.jg, s32[7]{0:T(128)S(1)} %convert_element_type.2.active, bf16[16,256,256]{2,1,0:T(8,128)(2,1)S(1)} %maximum_dynamic-update-slice_fusion.x, ...), custom_call_target="tpu_custom_call" | custom-call | flops 5637144576 | bytes 26214400 | tf_op jit(solution)/shard_map/forward/pallas_call | solution.py:68
  97.2 2.7 %collective-permute-start.16 = (bf16[256,2688]{1,0:T(8,128)(2,1)S(1)}, bf16[256,2688]{1,0:T(8,128)(2,1)S(1)}, u32[]{:S(2)}, u32[]{:S(2)}) collective-permute-start(bf16[256,2688]{1,0:T(8,128)(2,1)S(1)} %forward.1.act.refs_0_), channel_id=1, source_target_pairs={{0,96},{32,0},{64,32},{96,64},{1,97},{33,1},{65,33},{97,65},{2,98}... | collective-permute-start | bytes 4128776 | tf_op jit(solution)/shard_map/ppermute | solution.py:14
  99.9 14.2 %backward.1 = bf16[16,256,256]{2,1,0:T(8,128)(2,1)} custom-call(s32[16]{0:T(128)S(1)} %iota.14.js, bf16[256,2688]{1,0:T(8,128)(2,1)S(1)} %forward.1.act.refs_0_, bf16[4096,896]{1,0:T(8,128)(2,1)S(1)} %copy-done, bf16[4096,896]{1,0:T(8,128)(2,1)} %wu.3), custom_call_target="tpu_custom_call" | custom-call | flops 3758096384 | bytes 16777216 | tf_op jit(solution)/shard_map/backward/pallas_call | solution.py:111
  114.1 4.4 %all-to-all-start = ((bf16[16,256,256]{2,1,0:T(8,128)(2,1)}), bf16[16,256,256]{2,1,0:T(8,128)(2,1)}, u32[]{:S(2)}, u32[]{:S(2)}) async-start(bf16[16,256,256]{2,1,0:T(8,128)(2,1)} %backward.1), calls=%async_computation | async-start | bytes 4194304 | tf_op jit(solution)/shard_map/all_to_all | solution.py:275
  118.6 11.5 %collective-permute-start.20 = (bf16[256,2688]{1,0:T(8,128)(2,1)S(1)}, bf16[256,2688]{1,0:T(8,128)(2,1)}, u32[]{:S(2)}, u32[]{:S(2)}) collective-permute-start(bf16[256,2688]{1,0:T(8,128)(2,1)S(1)} %forward.1.act.refs_0_), channel_id=1, source_target_pairs={{0,16},{16,0},{1,17},{17,1},{2,18},{18,2},{3,19},{19,3},{4,20},{20... | collective-permute-start | bytes 4128776 | tf_op jit(solution)/shard_map/ppermute | solution.py:272
  132.9 2.6 %collective-permute-start.21 = (bf16[256,2688]{1,0:T(8,128)(2,1)S(1)}, bf16[256,2688]{1,0:T(8,128)(2,1)}, u32[]{:S(2)}, u32[]{:S(2)}) collective-permute-start(bf16[256,2688]{1,0:T(8,128)(2,1)S(1)} %collective-permute-done.16.refs_1_), channel_id=1, source_target_pairs={{0,16},{16,0},{1,17},{17,1},{2,18},{18,2},{3,19},{19,3},{4,20},{20... | collective-permute-start | bytes 4128776 | tf_op jit(solution)/shard_map/ppermute | solution.py:272
  135.5 11.5 %collective-permute-done.18.refs_3_ = bf16[128,2688]{1,0:T(8,128)(2,1)S(1)} collective-permute-done((bf16[128,2688]{1,0:T(8,128)(2,1)S(1)}, bf16[128,2688]{1,0:T(8,128)(2,1)S(1)}, u32[]{:S(2)}, u32[]{:S(2)}) %collective-permute-start.18) | collective-permute-done | bytes 688160 | tf_op jit(solution)/shard_map/ppermute | solution.py:14
  148.0 3.5 %collective-permute-start.24 = (bf16[128,2688]{1,0:T(8,128)(2,1)}, bf16[128,2688]{1,0:T(8,128)(2,1)}, u32[]{:S(2)}, u32[]{:S(2)}) collective-permute-start(bf16[128,2688]{1,0:T(8,128)(2,1)} %collective-permute-done.19.refs_4_), channel_id=1, source_target_pairs={{0,16},{16,0},{1,17},{17,1},{2,18},{18,2},{3,19},{19,3},{4,20},{20... | collective-permute-start | bytes 2064392 | tf_op jit(solution)/shard_map/ppermute | solution.py:272
  151.8 2.6 %reduce_sum.12 = bf16[256,256]{1,0:T(8,128)(2,1)} reduce(bf16[16,256,256]{2,1,0:T(8,128)(2,1)} %all-to-all-done, bf16[]{:T(256)} %constant.66.clone.1), dimensions={0}, to_apply=%region_1.2 | reduce | flops 983040 | bytes 2228226 | tf_op jit(solution)/shard_map/reduce_sum | solution.py:276
  154.4 12.4 %weight_grads.1 = (bf16[512,896]{1,0:T(8,128)(2,1)}, bf16[512,896]{1,0:T(8,128)(2,1)}, bf16[896,512]{1,0:T(8,128)(2,1)}) custom-call(s32[8,2]{1,0:T(8,128)S(1)} %copy.15.index, bf16[256,2688]{1,0:T(8,128)(2,1)S(1)} %forward.1.act.refs_0_, bf16[256,2688]{1,0:T(8,128)(2,1)S(1)} %collective-permute-done.16.refs_1_, ...), custom_call_target="tpu_custom_call" | custom-call | flops 5637144576 | bytes 15204352 | tf_op jit(solution)/shard_map/weight_grads/pallas_call | solution.py:204
  (93 shorter events, 12.6 us)
Async XLA Ops:
  7.2 147.2 %all-gather.3.cloned.1.call-start = ((), (), s32[]{:S(2)}) async-start(), calls=%async_computation.1 | async-start | bytes 4456448 | tf_op jit(solution)/shard_map/all_gather | solution.py:251
  8.3 10.9 %collective-permute-start.25 = (bf16[512,256]{1,0:T(8,128)(2,1)S(1)}, bf16[512,256]{1,0:T(8,128)(2,1)S(1)}, u32[]{:S(2)}, u32[]{:S(2)}) collective-permute-start(bf16[512,256]{1,0:T(8,128)(2,1)S(1)} %pad_maximum_fusion), channel_id=1, source_target_pairs={{0,0},{1,2},{2,16},{3,18},{4,32},{5,34},{6,48},{7,50},{8,64},{9,66... | collective-permute-start | bytes 786440 | tf_op jit(solution)/shard_map/ppermute | solution.py:250
  20.0 20.4 %collective-permute-start.8 = (bf16[1,256,256]{2,1,0:T(8,128)(2,1)}, bf16[1,256,256]{2,1,0:T(8,128)(2,1)S(1)}, u32[]{:S(2)}, u32[]{:S(2)}) collective-permute-start(bf16[1,256,256]{2,1,0:T(8,128)(2,1)} %bitcast.8), channel_id=1, source_target_pairs={{0,12},{4,0},{8,4},{12,8},{1,13},{5,1},{9,5},{13,9},{2,14},{6,2},{... | collective-permute-start | bytes 393224 | tf_op jit(solution)/shard_map/ppermute | solution.py:14
  34.4 8.8 %collective-permute-start.9 = (bf16[1,256,256]{2,1,0:T(8,128)(2,1)}, bf16[1,256,256]{2,1,0:T(8,128)(2,1)S(1)}, u32[]{:S(2)}, u32[]{:S(2)}) collective-permute-start(bf16[1,256,256]{2,1,0:T(8,128)(2,1)} %bitcast.9), channel_id=1, source_target_pairs={{0,4},{4,8},{8,12},{12,0},{1,5},{5,9},{9,13},{13,1},{2,6},{6,10},{... | collective-permute-start | bytes 393224 | tf_op jit(solution)/shard_map/ppermute | solution.py:14
  34.4 8.9 %collective-permute-start = (bf16[1,256,256]{2,1,0:T(8,128)(2,1)}, bf16[1,256,256]{2,1,0:T(8,128)(2,1)S(1)}, u32[]{:S(2)}, u32[]{:S(2)}) collective-permute-start(bf16[1,256,256]{2,1,0:T(8,128)(2,1)} %bitcast.11), channel_id=1, source_target_pairs={{0,3},{1,0},{2,1},{3,2},{4,7},{5,4},{6,5},{7,6},{8,11},{9,8},{10,9... | collective-permute-start | bytes 393224 | tf_op jit(solution)/shard_map/ppermute | solution.py:14
  35.2 10.2 %collective-permute-start.1 = (bf16[1,256,256]{2,1,0:T(8,128)(2,1)}, bf16[1,256,256]{2,1,0:T(8,128)(2,1)S(1)}, u32[]{:S(2)}, u32[]{:S(2)}) collective-permute-start(bf16[1,256,256]{2,1,0:T(8,128)(2,1)} %bitcast.12), channel_id=1, source_target_pairs={{0,1},{1,2},{2,3},{3,0},{4,5},{5,6},{6,7},{7,4},{8,9},{9,10},{10,1... | collective-permute-start | bytes 393224 | tf_op jit(solution)/shard_map/ppermute | solution.py:14
  43.3 6.7 %collective-permute-start.2 = (bf16[1,128,256]{2,1,0:T(8,128)(2,1)S(1)}, bf16[1,128,256]{2,1,0:T(8,128)(2,1)S(1)}, u32[]{:S(2)}, u32[]{:S(2)}) collective-permute-start(bf16[1,128,256]{2,1,0:T(8,128)(2,1)S(1)} %slice.40), channel_id=1, source_target_pairs={{0,3},{1,0},{2,1},{3,2},{4,7},{5,4},{6,5},{7,6},{8,11},{9,8},{10,9... | collective-permute-start | bytes 196616 | tf_op jit(solution)/shard_map/ppermute | solution.py:14
  47.7 12.7 %collective-permute-start.12 = (bf16[4,256,256]{2,1,0:T(8,128)(2,1)S(1)}, bf16[4,256,256]{2,1,0:T(8,128)(2,1)S(1)}, u32[]{:S(2)}, u32[]{:S(2)}) collective-permute-start(bf16[4,256,256]{2,1,0:T(8,128)(2,1)S(1)} %maximum_maximum_fusion.1), channel_id=1, source_target_pairs={{0,3},{1,0},{2,1},{3,2},{4,7},{5,4},{6,5},{7,6},{8,11},{9,8},{10,9... | collective-permute-start | bytes 1572872 | tf_op jit(solution)/shard_map/ppermute | solution.py:14
  50.0 13.0 %collective-permute-start.13 = (bf16[4,256,256]{2,1,0:T(8,128)(2,1)S(1)}, bf16[4,256,256]{2,1,0:T(8,128)(2,1)S(1)}, u32[]{:S(2)}, u32[]{:S(2)}) collective-permute-start(bf16[4,256,256]{2,1,0:T(8,128)(2,1)S(1)} %maximum_maximum_fusion.1), channel_id=1, source_target_pairs={{0,1},{1,2},{2,3},{3,0},{4,5},{5,6},{6,7},{7,4},{8,9},{9,10},{10,1... | collective-permute-start | bytes 1572872 | tf_op jit(solution)/shard_map/ppermute | solution.py:14
  50.2 12.9 %collective-permute-start.4 = (bf16[4,256,256]{2,1,0:T(8,128)(2,1)S(1)}, bf16[4,256,256]{2,1,0:T(8,128)(2,1)S(1)}, u32[]{:S(2)}, u32[]{:S(2)}) collective-permute-start(bf16[4,256,256]{2,1,0:T(8,128)(2,1)S(1)} %maximum_maximum_fusion), channel_id=1, source_target_pairs={{0,12},{4,0},{8,4},{12,8},{1,13},{5,1},{9,5},{13,9},{2,14},{6,2},{... | collective-permute-start | bytes 1572872 | tf_op jit(solution)/shard_map/ppermute | solution.py:14
  53.1 11.2 %collective-permute-start.5 = (bf16[4,256,256]{2,1,0:T(8,128)(2,1)S(1)}, bf16[4,256,256]{2,1,0:T(8,128)(2,1)S(1)}, u32[]{:S(2)}, u32[]{:S(2)}) collective-permute-start(bf16[4,256,256]{2,1,0:T(8,128)(2,1)S(1)} %maximum_maximum_fusion), channel_id=1, source_target_pairs={{0,4},{4,8},{8,12},{12,0},{1,5},{5,9},{9,13},{13,1},{2,6},{6,10},{... | collective-permute-start | bytes 1572872 | tf_op jit(solution)/shard_map/ppermute | solution.py:14
  60.4 11.9 %collective-permute-start.14 = (bf16[4,128,256]{2,1,0:T(8,128)(2,1)S(1)}, bf16[4,128,256]{2,1,0:T(8,128)(2,1)S(1)}, u32[]{:S(2)}, u32[]{:S(2)}) collective-permute-start(bf16[4,128,256]{2,1,0:T(8,128)(2,1)S(1)} %slice.46), channel_id=1, source_target_pairs={{0,3},{1,0},{2,1},{3,2},{4,7},{5,4},{6,5},{7,6},{8,11},{9,8},{10,9... | collective-permute-start | bytes 786440 | tf_op jit(solution)/shard_map/ppermute | solution.py:14
  63.0 11.8 %collective-permute-start.15 = (bf16[4,128,256]{2,1,0:T(8,128)(2,1)S(1)}, bf16[4,128,256]{2,1,0:T(8,128)(2,1)S(1)}, u32[]{:S(2)}, u32[]{:S(2)}) collective-permute-start(bf16[4,128,256]{2,1,0:T(8,128)(2,1)S(1)} %slice.47), channel_id=1, source_target_pairs={{0,1},{1,2},{2,3},{3,0},{4,5},{5,6},{6,7},{7,4},{8,9},{9,10},{10,1... | collective-permute-start | bytes 786440 | tf_op jit(solution)/shard_map/ppermute | solution.py:14
  63.1 11.7 %collective-permute-start.6 = (bf16[4,128,256]{2,1,0:T(8,128)(2,1)S(1)}, bf16[4,128,256]{2,1,0:T(8,128)(2,1)S(1)}, u32[]{:S(2)}, u32[]{:S(2)}) collective-permute-start(bf16[4,128,256]{2,1,0:T(8,128)(2,1)S(1)} %slice.42), channel_id=1, source_target_pairs={{0,12},{4,0},{8,4},{12,8},{1,13},{5,1},{9,5},{13,9},{2,14},{6,2},{... | collective-permute-start | bytes 786440 | tf_op jit(solution)/shard_map/ppermute | solution.py:14
  64.4 14.3 %collective-permute-start.7 = (bf16[4,128,256]{2,1,0:T(8,128)(2,1)S(1)}, bf16[4,128,256]{2,1,0:T(8,128)(2,1)S(1)}, u32[]{:S(2)}, u32[]{:S(2)}) collective-permute-start(bf16[4,128,256]{2,1,0:T(8,128)(2,1)S(1)} %slice.43), channel_id=1, source_target_pairs={{0,4},{4,8},{8,12},{12,0},{1,5},{5,9},{9,13},{13,1},{2,6},{6,10},{... | collective-permute-start | bytes 786440 | tf_op jit(solution)/shard_map/ppermute | solution.py:14
  97.2 32.8 %collective-permute-start.16 = (bf16[256,2688]{1,0:T(8,128)(2,1)S(1)}, bf16[256,2688]{1,0:T(8,128)(2,1)S(1)}, u32[]{:S(2)}, u32[]{:S(2)}) collective-permute-start(bf16[256,2688]{1,0:T(8,128)(2,1)S(1)} %forward.1.act.refs_0_), channel_id=1, source_target_pairs={{0,96},{32,0},{64,32},{96,64},{1,97},{33,1},{65,33},{97,65},{2,98}... | collective-permute-start | bytes 4128776 | tf_op jit(solution)/shard_map/ppermute | solution.py:14
  99.9 31.3 %collective-permute-start.17 = (bf16[256,2688]{1,0:T(8,128)(2,1)S(1)}, bf16[256,2688]{1,0:T(8,128)(2,1)}, u32[]{:S(2)}, u32[]{:S(2)}) collective-permute-start(bf16[256,2688]{1,0:T(8,128)(2,1)S(1)} %forward.1.act.refs_0_), channel_id=1, source_target_pairs={{0,32},{32,64},{64,96},{96,0},{1,33},{33,65},{65,97},{97,1},{2,34}... | collective-permute-start | bytes 4128776 | tf_op jit(solution)/shard_map/ppermute | solution.py:14
  114.1 37.7 %all-to-all-start = ((bf16[16,256,256]{2,1,0:T(8,128)(2,1)}), bf16[16,256,256]{2,1,0:T(8,128)(2,1)}, u32[]{:S(2)}, u32[]{:S(2)}) async-start(bf16[16,256,256]{2,1,0:T(8,128)(2,1)} %backward.1), calls=%async_computation | async-start | bytes 4194304 | tf_op jit(solution)/shard_map/all_to_all | solution.py:275
  118.6 35.8 %collective-permute-start.20 = (bf16[256,2688]{1,0:T(8,128)(2,1)S(1)}, bf16[256,2688]{1,0:T(8,128)(2,1)}, u32[]{:S(2)}, u32[]{:S(2)}) collective-permute-start(bf16[256,2688]{1,0:T(8,128)(2,1)S(1)} %forward.1.act.refs_0_), channel_id=1, source_target_pairs={{0,16},{16,0},{1,17},{17,1},{2,18},{18,2},{3,19},{19,3},{4,20},{20... | collective-permute-start | bytes 4128776 | tf_op jit(solution)/shard_map/ppermute | solution.py:272
  130.1 16.9 %collective-permute-start.18 = (bf16[128,2688]{1,0:T(8,128)(2,1)S(1)}, bf16[128,2688]{1,0:T(8,128)(2,1)S(1)}, u32[]{:S(2)}, u32[]{:S(2)}) collective-permute-start(bf16[128,2688]{1,0:T(8,128)(2,1)S(1)} %slice.48), channel_id=1, source_target_pairs={{0,96},{32,0},{64,32},{96,64},{1,97},{33,1},{65,33},{97,65},{2,98}... | collective-permute-start | bytes 2064392 | tf_op jit(solution)/shard_map/ppermute | solution.py:14
  132.3 15.7 %collective-permute-start.19 = (bf16[128,2688]{1,0:T(8,128)(2,1)S(1)}, bf16[128,2688]{1,0:T(8,128)(2,1)}, u32[]{:S(2)}, u32[]{:S(2)}) collective-permute-start(bf16[128,2688]{1,0:T(8,128)(2,1)S(1)} %slice.49), channel_id=1, source_target_pairs={{0,32},{32,64},{64,96},{96,0},{1,33},{33,65},{65,97},{97,1},{2,34}... | collective-permute-start | bytes 2064392 | tf_op jit(solution)/shard_map/ppermute | solution.py:14
  132.9 21.5 %collective-permute-start.21 = (bf16[256,2688]{1,0:T(8,128)(2,1)S(1)}, bf16[256,2688]{1,0:T(8,128)(2,1)}, u32[]{:S(2)}, u32[]{:S(2)}) collective-permute-start(bf16[256,2688]{1,0:T(8,128)(2,1)S(1)} %collective-permute-done.16.refs_1_), channel_id=1, source_target_pairs={{0,16},{16,0},{1,17},{17,1},{2,18},{18,2},{3,19},{19,3},{4,20},{20... | collective-permute-start | bytes 4128776 | tf_op jit(solution)/shard_map/ppermute | solution.py:272
  135.4 19.0 %collective-permute-start.22 = (bf16[256,2688]{1,0:T(8,128)(2,1)}, bf16[256,2688]{1,0:T(8,128)(2,1)}, u32[]{:S(2)}, u32[]{:S(2)}) collective-permute-start(bf16[256,2688]{1,0:T(8,128)(2,1)} %collective-permute-done.17.refs_2_), channel_id=1, source_target_pairs={{0,16},{16,0},{1,17},{17,1},{2,18},{18,2},{3,19},{19,3},{4,20},{20... | collective-permute-start | bytes 4128776 | tf_op jit(solution)/shard_map/ppermute | solution.py:272
  147.0 7.4 %collective-permute-start.23 = (bf16[128,2688]{1,0:T(8,128)(2,1)S(1)}, bf16[128,2688]{1,0:T(8,128)(2,1)}, u32[]{:S(2)}, u32[]{:S(2)}) collective-permute-start(bf16[128,2688]{1,0:T(8,128)(2,1)S(1)} %collective-permute-done.18.refs_3_), channel_id=1, source_target_pairs={{0,16},{16,0},{1,17},{17,1},{2,18},{18,2},{3,19},{19,3},{4,20},{20... | collective-permute-start | bytes 2064392 | tf_op jit(solution)/shard_map/ppermute | solution.py:272
  (8 other events, 120.7 us)
Sparse Core Ops, SparseCore 0:
  20.1 72.7 all-gather.2

commit v2 on v0

v2 whole, which is shorter than its diff:
```python
import jax
import jax.numpy as jnp
from jax import lax
from jax.experimental import pallas as pl
from jax.experimental.pallas import tpu as pltpu
from jax.sharding import Mesh, PartitionSpec as P

BLOCK = 128
RING = 4
OFFSETS = (0, 1, 3, 2)
MIB = 2**20

IN_VMEM = pl.BlockSpec(memory_space=pltpu.VMEM)
IN_SMEM = pl.BlockSpec(memory_space=pltpu.SMEM)
ANYWHERE = pl.BlockSpec(memory_space=pl.ANY)


def from_offset(value, axis, offset):
    return lax.ppermute(value, axis, [(i, (i - offset) % RING) for i in range(RING)])


def place_of(offset):
    offset = lax.rem(offset + RING, RING)
    return jnp.where(offset < 2, offset, 5 - offset)


def nn(a, b):
    return jnp.dot(a, b, preferred_element_type=jnp.float32)


def nt(a, b):
    return lax.dot_general(a, b, (((1,), (1,)), ((), ())), preferred_element_type=jnp.float32)


def tn(a, b):
    return lax.dot_general(a, b, (((0,), (0,)), ((), ())), preferred_element_type=jnp.float32)


def relay(value, *behind):
    def kernel(*refs):
        refs[-1][...] = refs[0][...]

    return pl.pallas_call(
        kernel,
        in_specs=[IN_VMEM] + [ANYWHERE] * len(behind),
        out_specs=IN_VMEM,
        out_shape=jax.ShapeDtypeStruct(value.shape, value.dtype),
        compiler_params=pltpu.CompilerParams(vmem_limit_bytes=4 * MIB),
        cost_estimate=pl.CostEstimate(
            flops=0, bytes_accessed=4 * value.size, transcendentals=0
        ),
        name="relay",
    )(value, *behind)


def halves(after, before, behind):
    rows, cols = after.shape
    half = rows // 2

    def kernel(after, before, behind, low, high, sems):
        copies = [
            pltpu.make_async_copy(after.at[pl.ds(0, half)], low, sems.at[0]),
            pltpu.make_async_copy(before.at[pl.ds(half, half)], high, sems.at[1]),
        ]
        for copy in copies:
            copy.start()
        for copy in copies:
            copy.wait()

    return pl.pallas_call(
        kernel,
        in_specs=[ANYWHERE] * 3,
        out_specs=[IN_VMEM] * 2,
        out_shape=[jax.ShapeDtypeStruct((half, cols), after.dtype)] * 2,
        scratch_shapes=[pltpu.SemaphoreType.DMA((2,))],
        compiler_params=pltpu.CompilerParams(vmem_limit_bytes=4 * MIB),
        cost_estimate=pl.CostEstimate(
            flops=0, bytes_accessed=4 * rows * cols, transcendentals=0
        ),
        name="halves",
    )(after, before, behind)


def group_buffers(depth, f_local, count):
    return [
        pltpu.VMEM((count, 4 * depth, f_local), jnp.bfloat16),
        pltpu.VMEM((count, 4 * depth, f_local), jnp.bfloat16),
        pltpu.VMEM((count, f_local, 4 * depth), jnp.bfloat16),
        pltpu.SemaphoreType.DMA((6 * count,)),
    ]


def fetch_group(coords, s, offset, weights, buffers):
    wg, wu, wd = weights
    wg_buf, wu_buf, wd_buf, sems = buffers
    wide = wg_buf.shape[1]
    depth = wide // 4
    row, col = lax.rem(coords[2] + offset, 4), lax.rem(coords[3] + offset, 4)
    rows = pl.ds(pl.multiple_of(row * wide, wide), wide)
    views = [(wg.at[rows], wg_buf.at[s]), (wu.at[rows], wu_buf.at[s])]
    for k in range(4):
        cols = pl.ds(pl.multiple_of((4 * k + col) * depth, depth), depth)
        views.append((wd.at[:, cols], wd_buf.at[s, :, pl.ds(k * depth, depth)]))
    copies = [
        pltpu.make_async_copy(source, target, sems.at[6 * s + j])
        for j, (source, target) in enumerate(views)
    ]
    for copy in copies:
        copy.start()
    return copies


def group_terms(coords, s, x, dy, copies, buffers):
    y, z = coords[2], coords[3]
    x = jnp.concatenate([x[place_of(k - z)] for k in range(4)], axis=1)
    copies[0].wait()
    yield nn(x, buffers[0][s])
    copies[1].wait()
    yield nn(x, buffers[1][s])
    dy = jnp.concatenate([dy[place_of(k - y)] for k in range(4)], axis=1)
    for copy in copies[2:]:
        copy.wait()
    yield nt(dy, buffers[2][s])


def forward_first(coords, x, dy, weights):
    rows, depth = x.shape[1:]
    f_local = weights[0].shape[1]

    def kernel(coords, x, dy, wg, wu, wd, *refs):
        outs, held, sems, buffers = refs[:3], refs[3], refs[4], refs[5:]
        loads = [
            pltpu.make_async_copy(piece, held.at[k], sems.at[k]) for k, piece in enumerate((x, dy))
        ]
        for load in loads:
            load.start()
        copies = fetch_group(coords, 0, 0, (wg, wu, wd), buffers)
        for load in loads:
            load.wait()
        for out, term in zip(outs, group_terms(coords, 0, held.at[0], held.at[1], copies, buffers)):
            out[...] = term

    return pl.pallas_call(
        kernel,
        in_specs=[IN_SMEM] + [ANYWHERE] * 5,
        out_specs=[IN_VMEM] * 3,
        out_shape=[jax.ShapeDtypeStruct((rows, f_local), jnp.float32)] * 3,
        scratch_shapes=[
            pltpu.VMEM((2, 4, rows, depth), jnp.bfloat16),
            pltpu.SemaphoreType.DMA((2,)),
        ]
        + group_buffers(depth, f_local, 1),
        compiler_params=pltpu.CompilerParams(vmem_limit_bytes=48 * MIB),
        cost_estimate=pl.CostEstimate(
            flops=24 * rows * depth * f_local,
            bytes_accessed=24 * depth * f_local,
            transcendentals=0,
        ),
        name="forward_first",
    )(coords, x, dy, *weights)


def forward_more(coords, offsets, xs, dys, weights, sums, active):
    count = len(offsets)
    rows, depth = xs[0].shape[1:]
    f_local = weights[0].shape[1]
    nblk = f_local // BLOCK
    last = active is not None

    def kernel(coords, *refs):
        on, refs = (refs[0], refs[1:]) if last else (None, refs)
        pieces, weights = refs[: 2 * count], refs[2 * count : 2 * count + 3]
        olds, refs = refs[2 * count + 3 : 2 * count + 6], refs[2 * count + 6 :]
        outs, refs = (refs[:1], refs[1:]) if last else (refs[:3], refs[3:])
        accs, old_bufs, held, sems, buffers = refs[:3], refs[3:6], refs[6], refs[7], refs[8:]
        groups = []
        for s, offset in enumerate(offsets):
            loads = [
                pltpu.make_async_copy(pieces[k], held.at[k], sems.at[k]) for k in (s, count + s)
            ]
            for load in loads:
                load.start()
            groups.append((loads, fetch_group(coords, s, offset, weights, buffers)))
        old_loads = [
            pltpu.make_async_copy(old, old_buf, sems.at[2 * count + k])
            for k, (old, old_buf) in enumerate(zip(olds, old_bufs))
        ]
        for load in old_loads:
            load.start()
        for s, (loads, copies) in enumerate(groups):
            for load in loads:
                load.wait()
            terms = group_terms(coords, s, held.at[s], held.at[count + s], copies, buffers)
            for acc, term in zip(accs, terms):
                acc[...] = term if s == 0 else acc[...] + term
        for load in old_loads:
            load.wait()
        if not last:
            for out, acc, old in zip(outs, accs, old_bufs):
                out[...] = acc[...] + old[...]
            return
        for b in range(nblk):
            cols = pl.ds(b * BLOCK, BLOCK)
            gate, up, hid = (acc[:, cols] + old[:, cols] for acc, old in zip(accs, old_bufs))
            logistic = jax.nn.sigmoid(gate)
            swish = gate * logistic
            values = (
                swish * up,
                hid * up * logistic * (1.0 + gate * (1.0 - logistic)),
                hid * swish,
            )
            for k, value in enumerate(values):
                outs[0][:, pl.ds(k * f_local + b * BLOCK, BLOCK)] = jnp.where(
                    on[b] > 0, value, 0.0
                ).astype(outs[0].dtype)

    act_shape = jax.ShapeDtypeStruct((rows, 3 * f_local), jnp.bfloat16)
    sum_shape = jax.ShapeDtypeStruct((rows, f_local), jnp.float32)
    return pl.pallas_call(
        kernel,
        in_specs=[IN_SMEM] * (2 if last else 1) + [ANYWHERE] * (2 * count + 6),
        out_specs=IN_VMEM if last else [IN_VMEM] * 3,
        out_shape=act_shape if last else [sum_shape] * 3,
        scratch_shapes=[pltpu.VMEM((rows, f_local), jnp.float32)] * 6
        + [
            pltpu.VMEM((2 * count, 4, rows, depth), jnp.bfloat16),
            pltpu.SemaphoreType.DMA((2 * count + 3,)),
        ]
        + group_buffers(depth, f_local, count),
        compiler_params=pltpu.CompilerParams(vmem_limit_bytes=48 * MIB),
        cost_estimate=pl.CostEstimate(
            flops=24 * count * rows * depth * f_local,
            bytes_accessed=24 * count * depth * f_local,
            transcendentals=rows * f_local if last else 0,
        ),
        name="forward_last" if last else "forward_near",
    )(coords, *([active] if last else []), *xs, *dys, *weights, *sums)


def backward(act, wg, wu):
    rows = act.shape[0]
    d_model, f_local = wg.shape
    n = 16
    depth = d_model // n
    wide = 4 * depth

    def kernel(act, wg, wu, out, wg_buf, wu_buf, sems):
        copies = []
        for i in range(4):
            at = pl.ds(i * wide, wide)
            copies.append(
                (
                    pltpu.make_async_copy(wg.at[at], wg_buf.at[at], sems.at[2 * i]),
                    pltpu.make_async_copy(wu.at[at], wu_buf.at[at], sems.at[2 * i + 1]),
                )
            )
        for pair in copies:
            for copy in pair:
                copy.start()
        d_gate, d_up = (act[:, pl.ds(k * f_local, f_local)] for k in (1, 2))
        for i, pair in enumerate(copies):
            at = pl.ds(i * wide, wide)
            for copy in pair:
                copy.wait()
            total = (nt(d_gate, wg_buf[at]) + nt(d_up, wu_buf[at])).astype(out.dtype)
            for k in range(4):
                out[4 * i + k] = total[:, k * depth : (k + 1) * depth]

    return pl.pallas_call(
        kernel,
        in_specs=[IN_VMEM] + [ANYWHERE] * 2,
        out_specs=IN_VMEM,
        out_shape=jax.ShapeDtypeStruct((n, rows, depth), jnp.bfloat16),
        scratch_shapes=[
            pltpu.VMEM(wg.shape, jnp.bfloat16),
            pltpu.VMEM(wu.shape, jnp.bfloat16),
            pltpu.SemaphoreType.DMA((8,)),
        ],
        compiler_params=pltpu.CompilerParams(vmem_limit_bytes=50 * MIB),
        cost_estimate=pl.CostEstimate(
            flops=4 * rows * d_model * f_local,
            bytes_accessed=4 * d_model * f_local,
            transcendentals=0,
        ),
        name="backward",
    )(act, wg, wu)


def weight_grads(coords, tiles, pieces):
    count, chunk = len(tiles), 4
    parts = [part for _, _, tile in tiles for part in tile]
    wide = parts[0].shape[1]
    rows = pieces.shape[1] // 2
    f_local = wide // 3
    depth = pieces.shape[2]
    cols = 2 * depth
    shapes = [(cols, f_local), (cols, f_local), (f_local, cols)]

    def kernel(coords, *refs):
        acts, refs = list(refs[: len(parts)]), refs[len(parts) :]
        pieces, outs, mark, accs, results = refs[0], refs[1:4], refs[4], refs[5:8], refs[8:11]
        act_buf, tok_buf, cot_buf, sems = refs[11:]
        mark[...] = jnp.zeros_like(mark)
        x, c = coords[0], coords[1]
        used = [0]

        def start(source, target):
            copy = pltpu.make_async_copy(source, target, sems.at[used[0]])
            used[0] += 1
            copy.start()
            return copy

        loads = []
        for t, (offset, other, tile) in enumerate(tiles):
            mine, at = [], t * rows
            for part in tile:
                mine.append(start(acts.pop(0), act_buf.at[pl.ds(at, part.shape[0])]))
                at += part.shape[0]
            core = 1 - c if other else c
            for h in range(2):
                piece = lax.rem(x + offset, RING) * RING + core + 2 * h
                for k, buf in enumerate((tok_buf, cot_buf)):
                    target = buf.at[pl.ds(t * rows, rows), pl.ds(h * depth, depth)]
                    mine.append(start(pieces.at[piece, pl.ds(k * rows, rows)], target))
            loads.append(mine)
        stores = []
        for t in range(0, count, chunk):
            for load in sum(loads[t : t + chunk], []):
                load.wait()
            at = pl.ds(t * rows, chunk * rows)
            for k in range(3):
                if k < 2:
                    term = tn(tok_buf[at], act_buf[at, pl.ds((k + 1) * f_local, f_local)])
                else:
                    term = tn(act_buf[at, pl.ds(0, f_local)], cot_buf[at])
                if t > 0:
                    term = accs[k][...] + term
                if t + chunk < count:
                    accs[k][...] = term
                else:
                    results[k][...] = term.astype(results[k].dtype)
                    stores.append(start(results[k], outs[k]))
        for store in stores:
            store.wait()

    return pl.pallas_call(
        kernel,
        in_specs=[IN_SMEM] + [ANYWHERE] * (len(parts) + 1),
        out_specs=[ANYWHERE] * 3 + [IN_VMEM],
        out_shape=[jax.ShapeDtypeStruct(shape, jnp.bfloat16) for shape in shapes + [(16, 128)]],
        scratch_shapes=[pltpu.VMEM(shape, jnp.float32) for shape in shapes]
        + [pltpu.VMEM(shape, jnp.bfloat16) for shape in shapes]
        + [
            pltpu.VMEM((count * rows, wide), jnp.bfloat16),
            pltpu.VMEM((count * rows, cols), jnp.bfloat16),
            pltpu.VMEM((count * rows, cols), jnp.bfloat16),
            pltpu.SemaphoreType.DMA((len(parts) + 4 * count + 3,)),
        ],
        compiler_params=pltpu.CompilerParams(vmem_limit_bytes=58 * MIB),
        cost_estimate=pl.CostEstimate(
            flops=4 * count * rows * depth * wide,
            bytes_accessed=2 * count * rows * (wide + 4 * depth),
            transcendentals=0,
        ),
        name="weight_grads",
    )(coords, *parts, pieces)


def sum_shares(shares, behind):
    n, rows, cols = shares.shape

    def kernel(shares, behind, out):
        total = shares[0].astype(jnp.float32)
        for k in range(1, n):
            total += shares[k].astype(jnp.float32)
        out[...] = total.astype(out.dtype)

    return pl.pallas_call(
        kernel,
        in_specs=[IN_VMEM, ANYWHERE],
        out_specs=IN_VMEM,
        out_shape=jax.ShapeDtypeStruct((rows, cols), shares.dtype),
        compiler_params=pltpu.CompilerParams(vmem_limit_bytes=8 * MIB),
        cost_estimate=pl.CostEstimate(
            flops=n * rows * cols, bytes_accessed=2 * n * rows * cols, transcendentals=0
        ),
        name="sum_shares",
    )(shares, behind)


def to_columns():
    order = [(x, c, y, z) for x in range(4) for c in range(2) for y in range(4) for z in range(4)]
    flat = lambda x, c, y, z: ((x * 2 + c) * 4 + y) * 4 + z
    return [(flat(x, c, y, z), flat(y, z // 2, x, z % 2 * 2 + c)) for x, c, y, z in order]


def per_device(tokens, grad_out, w_gate, w_up, w_down, active_ids, active_count):
    rows, depth = tokens.shape
    half = rows // 2
    f_local = w_gate.shape[1]
    nblk = f_local // BLOCK
    x, c, y, z = (lax.axis_index(a) for a in ("x", "c", "y", "z"))
    coords = jnp.stack([x, c, y, z]).astype(jnp.int32)

    tok, cot = tokens[None], grad_out[None]
    tok_near = [from_offset(tok, "z", o) for o in OFFSETS[1:]]
    cot_near = [from_offset(cot, "y", o) for o in OFFSETS[1:]]
    tok_row = jnp.concatenate([tok] + tok_near, axis=0)
    cot_row = jnp.concatenate([cot] + cot_near, axis=0)
    tok_after, tok_before = from_offset(tok_row, "y", 1), from_offset(tok_row, "y", 3)
    cot_after, cot_before = from_offset(cot_row, "z", 1), from_offset(cot_row, "z", 3)
    tok_low = from_offset(tok_after[:, :half], "y", 1)
    tok_high = from_offset(tok_before[:, half:], "y", 3)
    cot_low = from_offset(cot_after[:, :half], "z", 1)
    cot_high = from_offset(cot_before[:, half:], "z", 3)
    tok_far = jnp.concatenate([tok_low, tok_high], axis=1)
    cot_far = jnp.concatenate([cot_low, cot_high], axis=1)

    block_ids = (y * 4 + z) * nblk + jnp.arange(nblk, dtype=jnp.int32)
    listed = jnp.arange(active_ids.shape[1], dtype=jnp.int32) < active_count[0]
    matches = (active_ids[0][:, None] == block_ids[None, :]) & listed[:, None]
    active = jnp.any(matches, axis=0).astype(jnp.int32)

    weights = (w_gate, w_up, w_down)
    sums = forward_first(coords, tok_row, cot_row, weights)
    sums = forward_more(
        coords, [1, 3], [tok_after, tok_before], [cot_after, cot_before], weights, sums, None
    )
    both = jnp.concatenate([tokens, grad_out], axis=0)
    both = relay(both, tok_after, cot_after)
    turned = lax.ppermute(both, ("x", "c", "y", "z"), to_columns())
    pieces = lax.all_gather(relay(turned, tok_far, cot_far, sums[0]), ("y", "z"))

    act = forward_more(coords, [2], [tok_far], [cot_far], weights, sums, active)

    after, before = from_offset(act, "x", 1), from_offset(act, "x", 3)
    partial_dx = backward(act, w_gate, w_up)
    shares = lax.all_to_all(partial_dx, ("y", "z"), 0, 0)
    low, high = halves(after, before, partial_dx)
    far = [from_offset(low, "x", 1), from_offset(high, "x", 3)]
    swap = lambda a: lax.ppermute(a, "c", [(0, 1), (1, 0)])
    tiles = [(0, False, [act]), (1, False, [after]), (3, False, [before])]
    tiles += [(o, True, [swap(p) for p in tile]) for o, _, tile in tiles]
    tiles += [(2, False, far), (2, True, [swap(p) for p in far])]
    *grads, mark = weight_grads(coords, tiles, pieces)
    input_grad = sum_shares(shares, mark)
    return (input_grad, *grads)


def solution(mesh):
    fine = Mesh(mesh.devices.reshape(4, 2, 4, 4), ("x", "c", "y", "z"))
    dp, tensor = ("x", "c"), ("y", "z")
    in_specs = (
        P(dp, tensor),
        P(dp, tensor),
        P(None, tensor),
        P(None, tensor),
        P(tensor, None),
        P(dp, None),
        P(dp),
    )
    out_specs = (P(dp, tensor), P(dp, tensor), P(dp, tensor), P(tensor, dp))
    return jax.shard_map(
        per_device, mesh=fine, in_specs=in_specs, out_specs=out_specs, check_vma=False
    )
```

time: 351 us -> 151 us (0.43)
  waiting for transfers between devices: 262 us -> 24.4 us
  starting transfers between devices: 0.16 us -> 59.3 us
  matrix products: 45.5 us -> 0 us
  Pallas kernels: 0 us -> 40.6 us
  other arithmetic: 21 us -> 3.15 us
    reduce_scatter x2 -> x0, waiting for transfers between devices: 174 us -> none  [the longest x1 102 us: per_device(): lax.psum_scatter(jnp.concatenate([contract_rows(x_full, d_gate), contract...]
    all_gather x2 -> x1, waiting for transfers between devices: 86.7 us -> 0.01 us  [per_device(): lax.all_gather(relay(turned, tok_far, cot_far, sums[0]), ('y', 'z'))]
    ppermute x0 -> x24, starting transfers between devices: none -> 54.1 us  [the longest x18 34.5 us: from_offset(): lax.ppermute(value, axis, [(i, (i - offset) % RING) for i in range(RING)])]
    dot_general x8 -> x0, matrix products: 45.5 us -> none  [the longest x3 17.6 us: contract_rows(): lax.dot_general(left, right, (((0,), (0,)), ((), ())), preferred_element_...]
    pallas_call x0 -> x9, Pallas kernels: none -> 40.6 us  [the longest x1 12.3 us: weight_grads(): pl.pallas_call(kernel, in_specs=[IN_SMEM] + [ANYWHERE] * (len(parts) + 1)...]
    ppermute x0 -> x24, waiting for transfers between devices: none -> 24.4 us  [the longest x18 24.4 us: from_offset(): lax.ppermute(value, axis, [(i, (i - offset) % RING) for i in range(RING)])]
    concatenate x1 -> x3, other arithmetic: 20.1 us -> 2.87 us  [the longest x1 0.97 us: per_device(): tok_row = jnp.concatenate([tok] + tok_near, axis=0)]
    all_to_all x0 -> x1, starting transfers between devices: none -> 5.13 us  [per_device(): shares = lax.all_to_all(partial_dx, ('y', 'z'), 0, 0)]
  transfers between devices with their start and end apart: 4 -> 26, of which waited for: 4 -> 4; matrix products, arithmetic and copies ran while one was open for 9% -> 2% of each run, Pallas kernels for 0% -> 26%
where the time goes in v2:
time: 151 us
  starting transfers between devices  59.3 us (39%)
  Pallas kernels  40.6 us (27%)
  waiting for transfers between devices  24.4 us (16%)
  between operations  15 us (10%)
  local copies, waits for them, and re-layouts  8.42 us (6%)
  other arithmetic  3.15 us (2%)
    ppermute x18, starting transfers between devices, from_offset(): lax.ppermute(value, axis, [(i, (i - offset) % RING) for i in range(RING)])  34.5 us
    ppermute x18, waiting for transfers between devices, from_offset(): lax.ppermute(value, axis, [(i, (i - offset) % RING) for i in range(RING)])  24.4 us
    ppermute x5, starting transfers between devices, per_device(): swap = lambda a: lax.ppermute(a, 'c', [(0, 1), (1, 0)])  13.3 us
    pallas_call x1, Pallas kernels, weight_grads(): pl.pallas_call(kernel, in_specs=[IN_SMEM] + [ANYWHERE] * (len(parts) + 1)...  12.3 us
    pallas_call x2, Pallas kernels, forward_more(): pl.pallas_call(kernel, in_specs=[IN_SMEM] * (2 if last else 1) + [ANYWHER...  12.2 us
    pallas_call x1, Pallas kernels, backward(): pl.pallas_call(kernel, in_specs=[IN_VMEM] + [ANYWHERE] * 2, out_specs=IN_...  8.75 us
    unnamed x36, local copies, waits for them, and re-layouts  8.31 us
    ppermute x1, starting transfers between devices, per_device(): turned = lax.ppermute(both, ('x', 'c', 'y', 'z'), to_columns())  6.31 us
  transfers between devices with their start and end apart: 26, of which 4 were waited for; matrix products, arithmetic and copies ran while one was open for 2% of the time, Pallas kernels for 26%

profile of v2, /device:TPU:1, one launch (start us, length us, event | category | flops | bytes accessed | tf_op | source)
XLA Modules:
  0.0 150.9 jit_solution(9363332564691113535)
XLA Ops:
  7.2 3.8 %collective-permute-start.9 = (bf16[1,256,256]{2,1,0:T(8,128)(2,1)}, bf16[1,256,256]{2,1,0:T(8,128)(2,1)S(1)}, u32[]{:S(2)}, u32[]{:S(2)}) collective-permute-start(bf16[1,256,256]{2,1,0:T(8,128)(2,1)} %bitcast.14), channel_id=1, source_target_pairs={{0,8},{4,12},{8,0},{12,4},{1,9},{5,13},{9,1},{13,5},{2,10},{6,14},... | collective-permute-start | bytes 393224 | tf_op jit(solution)/shard_map/ppermute | solution.py:19
  11.4 2.3 %collective-permute-start.7 = (bf16[1,256,256]{2,1,0:T(8,128)(2,1)}, bf16[1,256,256]{2,1,0:T(8,128)(2,1)S(1)}, u32[]{:S(2)}, u32[]{:S(2)}) collective-permute-start(bf16[1,256,256]{2,1,0:T(8,128)(2,1)} %bitcast.16), channel_id=1, source_target_pairs={{0,12},{4,0},{8,4},{12,8},{1,13},{5,1},{9,5},{13,9},{2,14},{6,2},{... | collective-permute-start | bytes 393224 | tf_op jit(solution)/shard_map/ppermute | solution.py:19
  13.7 3.6 %collective-permute-start.2 = (bf16[1,256,256]{2,1,0:T(8,128)(2,1)}, bf16[1,256,256]{2,1,0:T(8,128)(2,1)S(1)}, u32[]{:S(2)}, u32[]{:S(2)}) collective-permute-start(bf16[1,256,256]{2,1,0:T(8,128)(2,1)} %bitcast.10), channel_id=1, source_target_pairs={{0,2},{1,3},{2,0},{3,1},{4,6},{5,7},{6,4},{7,5},{8,10},{9,11},{10,... | collective-permute-start | bytes 393224 | tf_op jit(solution)/shard_map/ppermute | solution.py:19
  18.1 1.9 %collective-permute-start = (bf16[1,256,256]{2,1,0:T(8,128)(2,1)}, bf16[1,256,256]{2,1,0:T(8,128)(2,1)S(1)}, u32[]{:S(2)}, u32[]{:S(2)}) collective-permute-start(bf16[1,256,256]{2,1,0:T(8,128)(2,1)} %bitcast.12), channel_id=1, source_target_pairs={{0,3},{1,0},{2,1},{3,2},{4,7},{5,4},{6,5},{7,6},{8,11},{9,8},{10,9... | collective-permute-start | bytes 393224 | tf_op jit(solution)/shard_map/ppermute | solution.py:19
  21.1 2.7 %collective-permute-start.10 = (bf16[4,256,256]{2,1,0:T(8,128)(2,1)S(1)}, bf16[4,256,256]{2,1,0:T(8,128)(2,1)S(1)}, u32[]{:S(2)}, u32[]{:S(2)}) collective-permute-start(bf16[4,256,256]{2,1,0:T(8,128)(2,1)S(1)} %pad_maximum_fusion.1.dy), channel_id=1, source_target_pairs={{0,3},{1,0},{2,1},{3,2},{4,7},{5,4},{6,5},{7,6},{8,11},{9,8},{10,9... | collective-permute-start | bytes 1572872 | tf_op jit(solution)/shard_map/ppermute | solution.py:19
  25.3 2.2 %collective-permute-start.3 = (bf16[4,256,256]{2,1,0:T(8,128)(2,1)S(1)}, bf16[4,256,256]{2,1,0:T(8,128)(2,1)S(1)}, u32[]{:S(2)}, u32[]{:S(2)}) collective-permute-start(bf16[4,256,256]{2,1,0:T(8,128)(2,1)S(1)} %pad_maximum_fusion.x), channel_id=1, source_target_pairs={{0,12},{4,0},{8,4},{12,8},{1,13},{5,1},{9,5},{13,9},{2,14},{6,2},{... | collective-permute-start | bytes 1572872 | tf_op jit(solution)/shard_map/ppermute | solution.py:19
  28.5 4.4 %forward_first.1 = (f32[256,896]{1,0:T(8,128)S(1)}, f32[256,896]{1,0:T(8,128)S(1)}, f32[256,896]{1,0:T(8,128)S(1)}) custom-call(s32[4]{0:T(128)S(1)} %pad_add_fusion.coords, bf16[4,256,256]{2,1,0:T(8,128)(2,1)S(1)} %pad_maximum_fusion.x, bf16[4,256,256]{2,1,0:T(8,128)(2,1)S(1)} %pad_maximum_fusion.1.dy, bf16[4096,896]{1,0:T(8,128)(2,1)} %wg.3, ...), custom_call_target="tpu_custom_call" | custom-call | flops 1409286144 | bytes 5505024 | tf_op jit(solution)/shard_map/forward_first/pallas_call | solution.py:143
  35.3 1.6 %collective-permute-start.11 = (bf16[4,128,256]{2,1,0:T(8,128)(2,1)S(1)}, bf16[4,128,256]{2,1,0:T(8,128)(2,1)S(1)}, u32[]{:S(2)}, u32[]{:S(2)}) collective-permute-start(bf16[4,128,256]{2,1,0:T(8,128)(2,1)S(1)} %slice.18), channel_id=1, source_target_pairs={{0,3},{1,0},{2,1},{3,2},{4,7},{5,4},{6,5},{7,6},{8,11},{9,8},{10,9... | collective-permute-start | bytes 786440 | tf_op jit(solution)/shard_map/ppermute | solution.py:19
  37.6 2.2 %collective-permute-start.4 = (bf16[4,128,256]{2,1,0:T(8,128)(2,1)S(1)}, bf16[4,128,256]{2,1,0:T(8,128)(2,1)S(1)}, u32[]{:S(2)}, u32[]{:S(2)}) collective-permute-start(bf16[4,128,256]{2,1,0:T(8,128)(2,1)S(1)} %slice.16), channel_id=1, source_target_pairs={{0,12},{4,0},{8,4},{12,8},{1,13},{5,1},{9,5},{13,9},{2,14},{6,2},{... | collective-permute-start | bytes 786440 | tf_op jit(solution)/shard_map/ppermute | solution.py:19
  39.8 6.3 %collective-permute-start.23 = (bf16[512,256]{1,0:T(8,128)(2,1)S(1)}, bf16[512,256]{1,0:T(8,128)(2,1)S(1)}, u32[]{:S(2)}, u32[]{:S(2)}) collective-permute-start(bf16[512,256]{1,0:T(8,128)(2,1)S(1)} %relay.2), channel_id=1, source_target_pairs={{0,0},{1,2},{2,16},{3,18},{4,32},{5,34},{6,48},{7,50},{8,64},{9,66... | collective-permute-start | bytes 786440 | tf_op jit(solution)/shard_map/ppermute | solution.py:431
  46.1 7.0 %forward_near.1 = (f32[256,896]{1,0:T(8,128)S(1)}, f32[256,896]{1,0:T(8,128)S(1)}, f32[256,896]{1,0:T(8,128)S(1)}) custom-call(s32[4]{0:T(128)S(1)} %pad_add_fusion.coords, bf16[4,256,256]{2,1,0:T(8,128)(2,1)S(1)} %collective-permute-done.3.refs_0_.refs_1_, bf16[4,256,256]{2,1,0:T(8,128)(2,1)S(1)} %collective-permute-done.5.refs_1_, ...), custom_call_target="tpu_custom_call" | custom-call | flops 2818572288 | bytes 11010048 | tf_op jit(solution)/shard_map/forward_near/pallas_call | solution.py:219
  58.4 5.2 %forward_last.1.act.refs_0_ = bf16[256,2688]{1,0:T(8,128)(2,1)S(1)} custom-call(s32[4]{0:T(128)S(1)} %pad_add_fusion.coords, s32[7]{0:T(128)S(1)} %convert_element_type.3.refs_0_, bf16[4,256,256]{2,1,0:T(8,128)(2,1)S(1)} %constant_dynamic-update-slice_fusion.refs_1_, bf16[4,256,256]{2,1,0:T(8,128)(2,1)S(1)} %constant_dynamic-update-slice_fusion.2.refs_2_, ...), custom_call_target="tpu_custom_call" | custom-call | flops 1409286144 | bytes 5505024 | tf_op jit(solution)/shard_map/forward_last/pallas_call | solution.py:219
  63.5 5.0 %collective-permute-start.15 = (bf16[256,2688]{1,0:T(8,128)(2,1)S(1)}, bf16[256,2688]{1,0:T(8,128)(2,1)}, u32[]{:S(2)}, u32[]{:S(2)}) collective-permute-start(bf16[256,2688]{1,0:T(8,128)(2,1)S(1)} %forward_last.1.act.refs_0_), channel_id=1, source_target_pairs={{0,32},{32,64},{64,96},{96,0},{1,33},{33,65},{65,97},{97,1},{2,34}... | collective-permute-start | bytes 4128776 | tf_op jit(solution)/shard_map/ppermute | solution.py:19
  68.6 2.5 %collective-permute-start.14 = (bf16[256,2688]{1,0:T(8,128)(2,1)S(1)}, bf16[256,2688]{1,0:T(8,128)(2,1)}, u32[]{:S(2)}, u32[]{:S(2)}) collective-permute-start(bf16[256,2688]{1,0:T(8,128)(2,1)S(1)} %forward_last.1.act.refs_0_), channel_id=1, source_target_pairs={{0,96},{32,0},{64,32},{96,64},{1,97},{33,1},{65,33},{97,65},{2,98}... | collective-permute-start | bytes 4128776 | tf_op jit(solution)/shard_map/ppermute | solution.py:19
  71.0 8.7 %backward.1.behind = bf16[16,256,256]{2,1,0:T(8,128)(2,1)} custom-call(bf16[256,2688]{1,0:T(8,128)(2,1)S(1)} %forward_last.1.act.refs_0_, bf16[4096,896]{1,0:T(8,128)(2,1)} %wg.3, bf16[4096,896]{1,0:T(8,128)(2,1)} %wu.3), custom_call_target="tpu_custom_call" | custom-call | flops 3758096384 | bytes 14680064 | tf_op jit(solution)/shard_map/backward/pallas_call | solution.py:269
  79.8 5.1 %all-to-all-start = ((bf16[16,256,256]{2,1,0:T(8,128)(2,1)}), bf16[16,256,256]{2,1,0:T(8,128)(2,1)S(1)}, u32[]{:S(2)}, u32[]{:S(2)}) async-start(bf16[16,256,256]{2,1,0:T(8,128)(2,1)} %backward.1.behind), calls=%async_computation | async-start | bytes 4194304 | tf_op jit(solution)/shard_map/all_to_all | solution.py:438
  85.0 4.0 %collective-permute-start.16 = (bf16[256,2688]{1,0:T(8,128)(2,1)S(1)}, bf16[256,2688]{1,0:T(8,128)(2,1)S(1)}, u32[]{:S(2)}, u32[]{:S(2)}) collective-permute-start(bf16[256,2688]{1,0:T(8,128)(2,1)S(1)} %forward_last.1.act.refs_0_), channel_id=1, source_target_pairs={{0,16},{16,0},{1,17},{17,1},{2,18},{18,2},{3,19},{19,3},{4,20},{20... | collective-permute-start | bytes 4128776 | tf_op jit(solution)/shard_map/ppermute | solution.py:441
  88.9 10.1 %collective-permute-done.15.before.refs_2_ = bf16[256,2688]{1,0:T(8,128)(2,1)} collective-permute-done((bf16[256,2688]{1,0:T(8,128)(2,1)S(1)}, bf16[256,2688]{1,0:T(8,128)(2,1)}, u32[]{:S(2)}, u32[]{:S(2)}) %collective-permute-start.15) | collective-permute-done | bytes 1376288 | tf_op jit(solution)/shard_map/ppermute | solution.py:19
  100.3 2.8 %collective-permute-start.19 = (bf16[128,2688]{1,0:T(8,128)(2,1)S(1)}, bf16[128,2688]{1,0:T(8,128)(2,1)S(1)}, u32[]{:S(2)}, u32[]{:S(2)}) collective-permute-start(bf16[128,2688]{1,0:T(8,128)(2,1)S(1)} %get-tuple-element.22), channel_id=1, source_target_pairs={{0,96},{32,0},{64,32},{96,64},{1,97},{33,1},{65,33},{97,65},{2,98}... | collective-permute-start | bytes 2064392 | tf_op jit(solution)/shard_map/ppermute | solution.py:19
  103.1 3.8 %collective-permute-start.18 = (bf16[256,2688]{1,0:T(8,128)(2,1)}, bf16[256,2688]{1,0:T(8,128)(2,1)S(1)}, u32[]{:S(2)}, u32[]{:S(2)}) collective-permute-start(bf16[256,2688]{1,0:T(8,128)(2,1)} %collective-permute-done.15.before.refs_2_), channel_id=1, source_target_pairs={{0,16},{16,0},{1,17},{17,1},{2,18},{18,2},{3,19},{19,3},{4,20},{20... | collective-permute-start | bytes 4128776 | tf_op jit(solution)/shard_map/ppermute | solution.py:441
  106.9 7.5 %collective-permute-done.19.refs_6_ = bf16[128,2688]{1,0:T(8,128)(2,1)S(1)} collective-permute-done((bf16[128,2688]{1,0:T(8,128)(2,1)S(1)}, bf16[128,2688]{1,0:T(8,128)(2,1)S(1)}, u32[]{:S(2)}, u32[]{:S(2)}) %collective-permute-start.19) | collective-permute-done | bytes 688160 | tf_op jit(solution)/shard_map/ppermute | solution.py:19
  114.4 4.3 %collective-permute-start.21 = (bf16[128,2688]{1,0:T(8,128)(2,1)S(1)}, bf16[128,2688]{1,0:T(8,128)(2,1)S(1)}, u32[]{:S(2)}, u32[]{:S(2)}) collective-permute-start(bf16[128,2688]{1,0:T(8,128)(2,1)S(1)} %collective-permute-done.19.refs_6_), channel_id=1, source_target_pairs={{0,16},{16,0},{1,17},{17,1},{2,18},{18,2},{3,19},{19,3},{4,20},{20... | collective-permute-start | bytes 2064392 | tf_op jit(solution)/shard_map/ppermute | solution.py:441
  118.7 5.9 %collective-permute-done.20.refs_7_ = bf16[128,2688]{1,0:T(8,128)(2,1)S(1)} collective-permute-done((bf16[128,2688]{1,0:T(8,128)(2,1)S(1)}, bf16[128,2688]{1,0:T(8,128)(2,1)S(1)}, u32[]{:S(2)}, u32[]{:S(2)}) %collective-permute-start.20) | collective-permute-done | bytes 688160 | tf_op jit(solution)/shard_map/ppermute | solution.py:19
  130.1 12.3 %weight_grads.1 = (bf16[512,896]{1,0:T(8,128)(2,1)}, bf16[512,896]{1,0:T(8,128)(2,1)}, bf16[896,512]{1,0:T(8,128)(2,1)}, bf16[16,128]{1,0:T(8,128)(2,1)}) custom-call(s32[4]{0:T(128)} %copy-done.7, bf16[256,2688]{1,0:T(8,128)(2,1)} %copy-done, bf16[256,2688]{1,0:T(8,128)(2,1)} %collective-permute-done.14.after.refs_1_, ...), custom_call_target="tpu_custom_call" | custom-call | flops 5637144576 | bytes 15204352 | tf_op jit(solution)/shard_map/weight_grads/pallas_call | solution.py:346
  (88 shorter events, 20.7 us)
Async XLA Ops:
  7.2 122.9 %all-gather.3.cloned.1.call-start = ((), (), s32[]{:S(2)}) async-start(), calls=%async_computation.1 | async-start | bytes 4456448 | tf_op jit(solution)/shard_map/all_gather | solution.py:432
  7.2 10.8 %collective-permute-start.9 = (bf16[1,256,256]{2,1,0:T(8,128)(2,1)}, bf16[1,256,256]{2,1,0:T(8,128)(2,1)S(1)}, u32[]{:S(2)}, u32[]{:S(2)}) collective-permute-start(bf16[1,256,256]{2,1,0:T(8,128)(2,1)} %bitcast.14), channel_id=1, source_target_pairs={{0,8},{4,12},{8,0},{12,4},{1,9},{5,13},{9,1},{13,5},{2,10},{6,14},... | collective-permute-start | bytes 393224 | tf_op jit(solution)/shard_map/ppermute | solution.py:19
  11.0 9.0 %collective-permute-start.8 = (bf16[1,256,256]{2,1,0:T(8,128)(2,1)}, bf16[1,256,256]{2,1,0:T(8,128)(2,1)S(1)}, u32[]{:S(2)}, u32[]{:S(2)}) collective-permute-start(bf16[1,256,256]{2,1,0:T(8,128)(2,1)} %bitcast.15), channel_id=1, source_target_pairs={{0,4},{4,8},{8,12},{12,0},{1,5},{5,9},{9,13},{13,1},{2,6},{6,10},{... | collective-permute-start | bytes 393224 | tf_op jit(solution)/shard_map/ppermute | solution.py:19
  11.4 8.6 %collective-permute-start.7 = (bf16[1,256,256]{2,1,0:T(8,128)(2,1)}, bf16[1,256,256]{2,1,0:T(8,128)(2,1)S(1)}, u32[]{:S(2)}, u32[]{:S(2)}) collective-permute-start(bf16[1,256,256]{2,1,0:T(8,128)(2,1)} %bitcast.16), channel_id=1, source_target_pairs={{0,12},{4,0},{8,4},{12,8},{1,13},{5,1},{9,5},{13,9},{2,14},{6,2},{... | collective-permute-start | bytes 393224 | tf_op jit(solution)/shard_map/ppermute | solution.py:19
  13.7 10.0 %collective-permute-start.2 = (bf16[1,256,256]{2,1,0:T(8,128)(2,1)}, bf16[1,256,256]{2,1,0:T(8,128)(2,1)S(1)}, u32[]{:S(2)}, u32[]{:S(2)}) collective-permute-start(bf16[1,256,256]{2,1,0:T(8,128)(2,1)} %bitcast.10), channel_id=1, source_target_pairs={{0,2},{1,3},{2,0},{3,1},{4,6},{5,7},{6,4},{7,5},{8,10},{9,11},{10,... | collective-permute-start | bytes 393224 | tf_op jit(solution)/shard_map/ppermute | solution.py:19
  17.3 6.4 %collective-permute-start.1 = (bf16[1,256,256]{2,1,0:T(8,128)(2,1)}, bf16[1,256,256]{2,1,0:T(8,128)(2,1)S(1)}, u32[]{:S(2)}, u32[]{:S(2)}) collective-permute-start(bf16[1,256,256]{2,1,0:T(8,128)(2,1)} %bitcast.11), channel_id=1, source_target_pairs={{0,1},{1,2},{2,3},{3,0},{4,5},{5,6},{6,7},{7,4},{8,9},{9,10},{10,1... | collective-permute-start | bytes 393224 | tf_op jit(solution)/shard_map/ppermute | solution.py:19
  21.0 12.7 %collective-permute-start.12 = (bf16[4,256,256]{2,1,0:T(8,128)(2,1)S(1)}, bf16[4,256,256]{2,1,0:T(8,128)(2,1)S(1)}, u32[]{:S(2)}, u32[]{:S(2)}) collective-permute-start(bf16[4,256,256]{2,1,0:T(8,128)(2,1)S(1)} %pad_maximum_fusion.1.dy), channel_id=1, source_target_pairs={{0,1},{1,2},{2,3},{3,0},{4,5},{5,6},{6,7},{7,4},{8,9},{9,10},{10,1... | collective-permute-start | bytes 1572872 | tf_op jit(solution)/shard_map/ppermute | solution.py:19
  21.1 14.2 %collective-permute-start.10 = (bf16[4,256,256]{2,1,0:T(8,128)(2,1)S(1)}, bf16[4,256,256]{2,1,0:T(8,128)(2,1)S(1)}, u32[]{:S(2)}, u32[]{:S(2)}) collective-permute-start(bf16[4,256,256]{2,1,0:T(8,128)(2,1)S(1)} %pad_maximum_fusion.1.dy), channel_id=1, source_target_pairs={{0,3},{1,0},{2,1},{3,2},{4,7},{5,4},{6,5},{7,6},{8,11},{9,8},{10,9... | collective-permute-start | bytes 1572872 | tf_op jit(solution)/shard_map/ppermute | solution.py:19
  24.7 12.2 %collective-permute-start.5 = (bf16[4,256,256]{2,1,0:T(8,128)(2,1)S(1)}, bf16[4,256,256]{2,1,0:T(8,128)(2,1)S(1)}, u32[]{:S(2)}, u32[]{:S(2)}) collective-permute-start(bf16[4,256,256]{2,1,0:T(8,128)(2,1)S(1)} %pad_maximum_fusion.x), channel_id=1, source_target_pairs={{0,4},{4,8},{8,12},{12,0},{1,5},{5,9},{9,13},{13,1},{2,6},{6,10},{... | collective-permute-start | bytes 1572872 | tf_op jit(solution)/shard_map/ppermute | solution.py:19
  25.3 12.2 %collective-permute-start.3 = (bf16[4,256,256]{2,1,0:T(8,128)(2,1)S(1)}, bf16[4,256,256]{2,1,0:T(8,128)(2,1)S(1)}, u32[]{:S(2)}, u32[]{:S(2)}) collective-permute-start(bf16[4,256,256]{2,1,0:T(8,128)(2,1)S(1)} %pad_maximum_fusion.x), channel_id=1, source_target_pairs={{0,12},{4,0},{8,4},{12,8},{1,13},{5,1},{9,5},{13,9},{2,14},{6,2},{... | collective-permute-start | bytes 1572872 | tf_op jit(solution)/shard_map/ppermute | solution.py:19
  33.7 19.5 %collective-permute-start.13 = (bf16[4,128,256]{2,1,0:T(8,128)(2,1)S(1)}, bf16[4,128,256]{2,1,0:T(8,128)(2,1)S(1)}, u32[]{:S(2)}, u32[]{:S(2)}) collective-permute-start(bf16[4,128,256]{2,1,0:T(8,128)(2,1)S(1)} %slice.19), channel_id=1, source_target_pairs={{0,1},{1,2},{2,3},{3,0},{4,5},{5,6},{6,7},{7,4},{8,9},{9,10},{10,1... | collective-permute-start | bytes 786440 | tf_op jit(solution)/shard_map/ppermute | solution.py:19
  35.3 17.9 %collective-permute-start.11 = (bf16[4,128,256]{2,1,0:T(8,128)(2,1)S(1)}, bf16[4,128,256]{2,1,0:T(8,128)(2,1)S(1)}, u32[]{:S(2)}, u32[]{:S(2)}) collective-permute-start(bf16[4,128,256]{2,1,0:T(8,128)(2,1)S(1)} %slice.18), channel_id=1, source_target_pairs={{0,3},{1,0},{2,1},{3,2},{4,7},{5,4},{6,5},{7,6},{8,11},{9,8},{10,9... | collective-permute-start | bytes 786440 | tf_op jit(solution)/shard_map/ppermute | solution.py:19
  36.9 16.4 %collective-permute-start.6 = (bf16[4,128,256]{2,1,0:T(8,128)(2,1)S(1)}, bf16[4,128,256]{2,1,0:T(8,128)(2,1)S(1)}, u32[]{:S(2)}, u32[]{:S(2)}) collective-permute-start(bf16[4,128,256]{2,1,0:T(8,128)(2,1)S(1)} %slice.17), channel_id=1, source_target_pairs={{0,4},{4,8},{8,12},{12,0},{1,5},{5,9},{9,13},{13,1},{2,6},{6,10},{... | collective-permute-start | bytes 786440 | tf_op jit(solution)/shard_map/ppermute | solution.py:19
  37.6 15.6 %collective-permute-start.4 = (bf16[4,128,256]{2,1,0:T(8,128)(2,1)S(1)}, bf16[4,128,256]{2,1,0:T(8,128)(2,1)S(1)}, u32[]{:S(2)}, u32[]{:S(2)}) collective-permute-start(bf16[4,128,256]{2,1,0:T(8,128)(2,1)S(1)} %slice.16), channel_id=1, source_target_pairs={{0,12},{4,0},{8,4},{12,8},{1,13},{5,1},{9,5},{13,9},{2,14},{6,2},{... | collective-permute-start | bytes 786440 | tf_op jit(solution)/shard_map/ppermute | solution.py:19
  39.8 14.3 %collective-permute-start.23 = (bf16[512,256]{1,0:T(8,128)(2,1)S(1)}, bf16[512,256]{1,0:T(8,128)(2,1)S(1)}, u32[]{:S(2)}, u32[]{:S(2)}) collective-permute-start(bf16[512,256]{1,0:T(8,128)(2,1)S(1)} %relay.2), channel_id=1, source_target_pairs={{0,0},{1,2},{2,16},{3,18},{4,32},{5,34},{6,48},{7,50},{8,64},{9,66... | collective-permute-start | bytes 786440 | tf_op jit(solution)/shard_map/ppermute | solution.py:431
  63.5 35.4 %collective-permute-start.15 = (bf16[256,2688]{1,0:T(8,128)(2,1)S(1)}, bf16[256,2688]{1,0:T(8,128)(2,1)}, u32[]{:S(2)}, u32[]{:S(2)}) collective-permute-start(bf16[256,2688]{1,0:T(8,128)(2,1)S(1)} %forward_last.1.act.refs_0_), channel_id=1, source_target_pairs={{0,32},{32,64},{64,96},{96,0},{1,33},{33,65},{65,97},{97,1},{2,34}... | collective-permute-start | bytes 4128776 | tf_op jit(solution)/shard_map/ppermute | solution.py:19
  68.6 30.4 %collective-permute-start.14 = (bf16[256,2688]{1,0:T(8,128)(2,1)S(1)}, bf16[256,2688]{1,0:T(8,128)(2,1)}, u32[]{:S(2)}, u32[]{:S(2)}) collective-permute-start(bf16[256,2688]{1,0:T(8,128)(2,1)S(1)} %forward_last.1.act.refs_0_), channel_id=1, source_target_pairs={{0,96},{32,0},{64,32},{96,64},{1,97},{33,1},{65,33},{97,65},{2,98}... | collective-permute-start | bytes 4128776 | tf_op jit(solution)/shard_map/ppermute | solution.py:19
  79.8 62.7 %all-to-all-start = ((bf16[16,256,256]{2,1,0:T(8,128)(2,1)}), bf16[16,256,256]{2,1,0:T(8,128)(2,1)S(1)}, u32[]{:S(2)}, u32[]{:S(2)}) async-start(bf16[16,256,256]{2,1,0:T(8,128)(2,1)} %backward.1.behind), calls=%async_computation | async-start | bytes 4194304 | tf_op jit(solution)/shard_map/all_to_all | solution.py:438
  85.0 41.0 %collective-permute-start.16 = (bf16[256,2688]{1,0:T(8,128)(2,1)S(1)}, bf16[256,2688]{1,0:T(8,128)(2,1)S(1)}, u32[]{:S(2)}, u32[]{:S(2)}) collective-permute-start(bf16[256,2688]{1,0:T(8,128)(2,1)S(1)} %forward_last.1.act.refs_0_), channel_id=1, source_target_pairs={{0,16},{16,0},{1,17},{17,1},{2,18},{18,2},{3,19},{19,3},{4,20},{20... | collective-permute-start | bytes 4128776 | tf_op jit(solution)/shard_map/ppermute | solution.py:441
  100.3 14.1 %collective-permute-start.19 = (bf16[128,2688]{1,0:T(8,128)(2,1)S(1)}, bf16[128,2688]{1,0:T(8,128)(2,1)S(1)}, u32[]{:S(2)}, u32[]{:S(2)}) collective-permute-start(bf16[128,2688]{1,0:T(8,128)(2,1)S(1)} %get-tuple-element.22), channel_id=1, source_target_pairs={{0,96},{32,0},{64,32},{96,64},{1,97},{33,1},{65,33},{97,65},{2,98}... | collective-permute-start | bytes 2064392 | tf_op jit(solution)/shard_map/ppermute | solution.py:19
  103.1 23.9 %collective-permute-start.18 = (bf16[256,2688]{1,0:T(8,128)(2,1)}, bf16[256,2688]{1,0:T(8,128)(2,1)S(1)}, u32[]{:S(2)}, u32[]{:S(2)}) collective-permute-start(bf16[256,2688]{1,0:T(8,128)(2,1)} %collective-permute-done.15.before.refs_2_), channel_id=1, source_target_pairs={{0,16},{16,0},{1,17},{17,1},{2,18},{18,2},{3,19},{19,3},{4,20},{20... | collective-permute-start | bytes 4128776 | tf_op jit(solution)/shard_map/ppermute | solution.py:441
  106.9 21.2 %collective-permute-start.17 = (bf16[256,2688]{1,0:T(8,128)(2,1)}, bf16[256,2688]{1,0:T(8,128)(2,1)S(1)}, u32[]{:S(2)}, u32[]{:S(2)}) collective-permute-start(bf16[256,2688]{1,0:T(8,128)(2,1)} %collective-permute-done.14.after.refs_1_), channel_id=1, source_target_pairs={{0,16},{16,0},{1,17},{17,1},{2,18},{18,2},{3,19},{19,3},{4,20},{20... | collective-permute-start | bytes 4128776 | tf_op jit(solution)/shard_map/ppermute | solution.py:441
  106.9 17.8 %collective-permute-start.20 = (bf16[128,2688]{1,0:T(8,128)(2,1)S(1)}, bf16[128,2688]{1,0:T(8,128)(2,1)S(1)}, u32[]{:S(2)}, u32[]{:S(2)}) collective-permute-start(bf16[128,2688]{1,0:T(8,128)(2,1)S(1)} %get-tuple-element.23), channel_id=1, source_target_pairs={{0,32},{32,64},{64,96},{96,0},{1,33},{33,65},{65,97},{97,1},{2,34}... | collective-permute-start | bytes 2064392 | tf_op jit(solution)/shard_map/ppermute | solution.py:19
  114.4 14.8 %collective-permute-start.21 = (bf16[128,2688]{1,0:T(8,128)(2,1)S(1)}, bf16[128,2688]{1,0:T(8,128)(2,1)S(1)}, u32[]{:S(2)}, u32[]{:S(2)}) collective-permute-start(bf16[128,2688]{1,0:T(8,128)(2,1)S(1)} %collective-permute-done.19.refs_6_), channel_id=1, source_target_pairs={{0,16},{16,0},{1,17},{17,1},{2,18},{18,2},{3,19},{19,3},{4,20},{20... | collective-permute-start | bytes 2064392 | tf_op jit(solution)/shard_map/ppermute | solution.py:441
  (19 other events, 139.2 us)
Sparse Core Ops, SparseCore 0:
  55.2 74.4 all-gather.2

commit v3 on v2

--- a/solution.py
+++ b/solution.py
@@ -287,7 +287,7 @@
 
 
 def weight_grads(coords, tiles, pieces):
-    count, chunk = len(tiles), 4
+    count, chunks = len(tiles), (1, 3, 4)
     parts = [part for _, _, tile in tiles for part in tile]
     wide = parts[0].shape[1]
     rows = pieces.shape[1] // 2
@@ -324,7 +324,7 @@
                     mine.append(start(pieces.at[piece, pl.ds(k * rows, rows)], target))
             loads.append(mine)
         stores = []
-        for t in range(0, count, chunk):
+        for t, chunk in zip((0, 1, 4), chunks):
             for load in sum(loads[t : t + chunk], []):
                 load.wait()
             at = pl.ds(t * rows, chunk * rows)
@@ -427,7 +427,6 @@
         coords, [1, 3], [tok_after, tok_before], [cot_after, cot_before], weights, sums, None
     )
     both = jnp.concatenate([tokens, grad_out], axis=0)
-    both = relay(both, tok_after, cot_after)
     turned = lax.ppermute(both, ("x", "c", "y", "z"), to_columns())
     pieces = lax.all_gather(relay(turned, tok_far, cot_far, sums[0]), ("y", "z"))
 

time: 151 us -> 149 us (0.987)
  waiting for transfers between devices: 24.4 us -> 13.3 us
  starting transfers between devices: 59.3 us -> 69.2 us
    ppermute x18, waiting for transfers between devices: 24.4 us -> 13.3 us  [from_offset(): lax.ppermute(value, axis, [(i, (i - offset) % RING) for i in range(RING)])]
    ppermute x5, starting transfers between devices: 13.3 us -> 24.1 us  [per_device(): swap = lambda a: lax.ppermute(a, 'c', [(0, 1), (1, 0)])]
    ppermute x18, starting transfers between devices: 34.5 us -> 31.4 us  [from_offset(): lax.ppermute(value, axis, [(i, (i - offset) % RING) for i in range(RING)])]
    all_to_all x1, starting transfers between devices: 5.13 us -> 6.69 us  [per_device(): shares = lax.all_to_all(partial_dx, ('y', 'z'), 0, 0)]
    unnamed x36 -> x38, local copies, waits for them, and re-layouts: 8.31 us -> 8.33 us
  transfers between devices with their start and end apart: 26 -> 26, of which waited for: 4 -> 2; matrix products, arithmetic and copies ran while one was open for 2% -> 2% of each run, Pallas kernels for 26% -> 26%
where the time goes in v3:
time: 149 us
  starting transfers between devices  69.2 us (46%)
  Pallas kernels  39.7 us (27%)
  between operations  15 us (10%)
  waiting for transfers between devices  13.3 us (9%)
  local copies, waits for them, and re-layouts  8.44 us (6%)
  other arithmetic  2.95 us (2%)
    ppermute x18, starting transfers between devices, from_offset(): lax.ppermute(value, axis, [(i, (i - offset) % RING) for i in range(RING)])  31.4 us
    ppermute x5, starting transfers between devices, per_device(): swap = lambda a: lax.ppermute(a, 'c', [(0, 1), (1, 0)])  24.1 us
    ppermute x18, waiting for transfers between devices, from_offset(): lax.ppermute(value, axis, [(i, (i - offset) % RING) for i in range(RING)])  13.3 us
    pallas_call x2, Pallas kernels, forward_more(): pl.pallas_call(kernel, in_specs=[IN_SMEM] * (2 if last else 1) + [ANYWHER...  12.2 us
    pallas_call x1, Pallas kernels, weight_grads(): pl.pallas_call(kernel, in_specs=[IN_SMEM] + [ANYWHERE] * (len(parts) + 1)...  11.6 us
    pallas_call x1, Pallas kernels, backward(): pl.pallas_call(kernel, in_specs=[IN_VMEM] + [ANYWHERE] * 2, out_specs=IN_...  8.61 us
    unnamed x38, local copies, waits for them, and re-layouts  8.33 us
    ppermute x1, starting transfers between devices, per_device(): turned = lax.ppermute(both, ('x', 'c', 'y', 'z'), to_columns())  6.89 us
  transfers between devices with their start and end apart: 26, of which 2 were waited for; matrix products, arithmetic and copies ran while one was open for 2% of the time, Pallas kernels for 26%

profile of v3, /device:TPU:1, one launch (start us, length us, event | category | flops | bytes accessed | tf_op | source)
XLA Modules:
  0.0 148.6 jit_solution(869885726295325145)
XLA Ops:
  7.2 3.8 %collective-permute-start.9 = (bf16[1,256,256]{2,1,0:T(8,128)(2,1)}, bf16[1,256,256]{2,1,0:T(8,128)(2,1)S(1)}, u32[]{:S(2)}, u32[]{:S(2)}) collective-permute-start(bf16[1,256,256]{2,1,0:T(8,128)(2,1)} %bitcast.14), channel_id=1, source_target_pairs={{0,8},{4,12},{8,0},{12,4},{1,9},{5,13},{9,1},{13,5},{2,10},{6,14},... | collective-permute-start | bytes 393224 | tf_op jit(solution)/shard_map/ppermute | solution.py:19
  11.5 2.3 %collective-permute-start.7 = (bf16[1,256,256]{2,1,0:T(8,128)(2,1)}, bf16[1,256,256]{2,1,0:T(8,128)(2,1)S(1)}, u32[]{:S(2)}, u32[]{:S(2)}) collective-permute-start(bf16[1,256,256]{2,1,0:T(8,128)(2,1)} %bitcast.16), channel_id=1, source_target_pairs={{0,12},{4,0},{8,4},{12,8},{1,13},{5,1},{9,5},{13,9},{2,14},{6,2},{... | collective-permute-start | bytes 393224 | tf_op jit(solution)/shard_map/ppermute | solution.py:19
  13.7 3.6 %collective-permute-start.2 = (bf16[1,256,256]{2,1,0:T(8,128)(2,1)}, bf16[1,256,256]{2,1,0:T(8,128)(2,1)S(1)}, u32[]{:S(2)}, u32[]{:S(2)}) collective-permute-start(bf16[1,256,256]{2,1,0:T(8,128)(2,1)} %bitcast.10), channel_id=1, source_target_pairs={{0,2},{1,3},{2,0},{3,1},{4,6},{5,7},{6,4},{7,5},{8,10},{9,11},{10,... | collective-permute-start | bytes 393224 | tf_op jit(solution)/shard_map/ppermute | solution.py:19
  18.1 1.9 %collective-permute-start = (bf16[1,256,256]{2,1,0:T(8,128)(2,1)}, bf16[1,256,256]{2,1,0:T(8,128)(2,1)S(1)}, u32[]{:S(2)}, u32[]{:S(2)}) collective-permute-start(bf16[1,256,256]{2,1,0:T(8,128)(2,1)} %bitcast.12), channel_id=1, source_target_pairs={{0,3},{1,0},{2,1},{3,2},{4,7},{5,4},{6,5},{7,6},{8,11},{9,8},{10,9... | collective-permute-start | bytes 393224 | tf_op jit(solution)/shard_map/ppermute | solution.py:19
  21.1 2.7 %collective-permute-start.10 = (bf16[4,256,256]{2,1,0:T(8,128)(2,1)S(1)}, bf16[4,256,256]{2,1,0:T(8,128)(2,1)S(1)}, u32[]{:S(2)}, u32[]{:S(2)}) collective-permute-start(bf16[4,256,256]{2,1,0:T(8,128)(2,1)S(1)} %pad_maximum_fusion.1.dy), channel_id=1, source_target_pairs={{0,3},{1,0},{2,1},{3,2},{4,7},{5,4},{6,5},{7,6},{8,11},{9,8},{10,9... | collective-permute-start | bytes 1572872 | tf_op jit(solution)/shard_map/ppermute | solution.py:19
  25.3 2.2 %collective-permute-start.3 = (bf16[4,256,256]{2,1,0:T(8,128)(2,1)S(1)}, bf16[4,256,256]{2,1,0:T(8,128)(2,1)S(1)}, u32[]{:S(2)}, u32[]{:S(2)}) collective-permute-start(bf16[4,256,256]{2,1,0:T(8,128)(2,1)S(1)} %pad_maximum_fusion.x), channel_id=1, source_target_pairs={{0,12},{4,0},{8,4},{12,8},{1,13},{5,1},{9,5},{13,9},{2,14},{6,2},{... | collective-permute-start | bytes 1572872 | tf_op jit(solution)/shard_map/ppermute | solution.py:19
  28.2 6.9 %collective-permute-start.23 = (bf16[512,256]{1,0:T(8,128)(2,1)}, bf16[512,256]{1,0:T(8,128)(2,1)S(1)}, u32[]{:S(2)}, u32[]{:S(2)}) collective-permute-start(bf16[512,256]{1,0:T(8,128)(2,1)} %pad_maximum_fusion.2), channel_id=1, source_target_pairs={{0,0},{1,2},{2,16},{3,18},{4,32},{5,34},{6,48},{7,50},{8,64},{9,66... | collective-permute-start | bytes 786440 | tf_op jit(solution)/shard_map/ppermute | solution.py:430
  35.2 4.4 %forward_first.1 = (f32[256,896]{1,0:T(8,128)S(1)}, f32[256,896]{1,0:T(8,128)S(1)}, f32[256,896]{1,0:T(8,128)S(1)}) custom-call(s32[4]{0:T(128)S(1)} %pad_add_fusion.coords, bf16[4,256,256]{2,1,0:T(8,128)(2,1)S(1)} %pad_maximum_fusion.x, bf16[4,256,256]{2,1,0:T(8,128)(2,1)S(1)} %pad_maximum_fusion.1.dy, bf16[4096,896]{1,0:T(8,128)(2,1)} %wg.3, ...), custom_call_target="tpu_custom_call" | custom-call | flops 1409286144 | bytes 5505024 | tf_op jit(solution)/shard_map/forward_first/pallas_call | solution.py:143
  39.7 1.5 collective-permute-start.13
  41.1 1.3 collective-permute-start.11
  42.5 2.2 %collective-permute-start.6 = (bf16[4,128,256]{2,1,0:T(8,128)(2,1)S(1)}, bf16[4,128,256]{2,1,0:T(8,128)(2,1)S(1)}, u32[]{:S(2)}, u32[]{:S(2)}) collective-permute-start(bf16[4,128,256]{2,1,0:T(8,128)(2,1)S(1)} %slice.17), channel_id=1, source_target_pairs={{0,4},{4,8},{8,12},{12,0},{1,5},{5,9},{9,13},{13,1},{2,6},{6,10},{... | collective-permute-start | bytes 786440 | tf_op jit(solution)/shard_map/ppermute | solution.py:19
  44.7 2.8 %collective-permute-start.4 = (bf16[4,128,256]{2,1,0:T(8,128)(2,1)S(1)}, bf16[4,128,256]{2,1,0:T(8,128)(2,1)S(1)}, u32[]{:S(2)}, u32[]{:S(2)}) collective-permute-start(bf16[4,128,256]{2,1,0:T(8,128)(2,1)S(1)} %slice.16), channel_id=1, source_target_pairs={{0,12},{4,0},{8,4},{12,8},{1,13},{5,1},{9,5},{13,9},{2,14},{6,2},{... | collective-permute-start | bytes 786440 | tf_op jit(solution)/shard_map/ppermute | solution.py:19
  47.5 7.0 %forward_near.1 = (f32[256,896]{1,0:T(8,128)S(1)}, f32[256,896]{1,0:T(8,128)S(1)}, f32[256,896]{1,0:T(8,128)S(1)}) custom-call(s32[4]{0:T(128)S(1)} %pad_add_fusion.coords, bf16[4,256,256]{2,1,0:T(8,128)(2,1)S(1)} %collective-permute-done.3.refs_0_, bf16[4,256,256]{2,1,0:T(8,128)(2,1)S(1)} %collective-permute-done.5.refs_1_, ...), custom_call_target="tpu_custom_call" | custom-call | flops 2818572288 | bytes 11010048 | tf_op jit(solution)/shard_map/forward_near/pallas_call | solution.py:219
  59.7 5.2 %forward_last.1.act.refs_0_ = bf16[256,2688]{1,0:T(8,128)(2,1)S(1)} custom-call(s32[4]{0:T(128)S(1)} %pad_add_fusion.coords, s32[7]{0:T(128)S(1)} %convert_element_type.3.refs_0_, bf16[4,256,256]{2,1,0:T(8,128)(2,1)S(1)} %constant_dynamic-update-slice_fusion.refs_1_, bf16[4,256,256]{2,1,0:T(8,128)(2,1)S(1)} %constant_dynamic-update-slice_fusion.2.refs_2_, ...), custom_call_target="tpu_custom_call" | custom-call | flops 1409286144 | bytes 5505024 | tf_op jit(solution)/shard_map/forward_last/pallas_call | solution.py:219
  65.0 2.7 %collective-permute-start.14 = (bf16[256,2688]{1,0:T(8,128)(2,1)S(1)}, bf16[256,2688]{1,0:T(8,128)(2,1)}, u32[]{:S(2)}, u32[]{:S(2)}) collective-permute-start(bf16[256,2688]{1,0:T(8,128)(2,1)S(1)} %forward_last.1.act.refs_0_), channel_id=1, source_target_pairs={{0,96},{32,0},{64,32},{96,64},{1,97},{33,1},{65,33},{97,65},{2,98}... | collective-permute-start | bytes 4128776 | tf_op jit(solution)/shard_map/ppermute | solution.py:19
  67.6 8.6 %backward.1.behind = bf16[16,256,256]{2,1,0:T(8,128)(2,1)} custom-call(bf16[256,2688]{1,0:T(8,128)(2,1)S(1)} %forward_last.1.act.refs_0_, bf16[4096,896]{1,0:T(8,128)(2,1)} %wg.3, bf16[4096,896]{1,0:T(8,128)(2,1)} %wu.3), custom_call_target="tpu_custom_call" | custom-call | flops 3758096384 | bytes 14680064 | tf_op jit(solution)/shard_map/backward/pallas_call | solution.py:269
  76.3 6.7 %all-to-all-start = ((bf16[16,256,256]{2,1,0:T(8,128)(2,1)}), bf16[16,256,256]{2,1,0:T(8,128)(2,1)S(1)}, u32[]{:S(2)}, u32[]{:S(2)}) async-start(bf16[16,256,256]{2,1,0:T(8,128)(2,1)} %backward.1.behind), calls=%async_computation | async-start | bytes 4194304 | tf_op jit(solution)/shard_map/all_to_all | solution.py:437
  83.0 4.4 %collective-permute-start.16 = (bf16[256,2688]{1,0:T(8,128)(2,1)S(1)}, bf16[256,2688]{1,0:T(8,128)(2,1)S(1)}, u32[]{:S(2)}, u32[]{:S(2)}) collective-permute-start(bf16[256,2688]{1,0:T(8,128)(2,1)S(1)} %forward_last.1.act.refs_0_), channel_id=1, source_target_pairs={{0,16},{16,0},{1,17},{17,1},{2,18},{18,2},{3,19},{19,3},{4,20},{20... | collective-permute-start | bytes 4128776 | tf_op jit(solution)/shard_map/ppermute | solution.py:440
  87.4 3.9 %collective-permute-done.15.before.refs_2_ = bf16[256,2688]{1,0:T(8,128)(2,1)} collective-permute-done((bf16[256,2688]{1,0:T(8,128)(2,1)S(1)}, bf16[256,2688]{1,0:T(8,128)(2,1)}, u32[]{:S(2)}, u32[]{:S(2)}) %collective-permute-start.15) | collective-permute-done | bytes 1376288 | tf_op jit(solution)/shard_map/ppermute | solution.py:19
  92.6 2.7 %collective-permute-start.19 = (bf16[128,2688]{1,0:T(8,128)(2,1)S(1)}, bf16[128,2688]{1,0:T(8,128)(2,1)S(1)}, u32[]{:S(2)}, u32[]{:S(2)}) collective-permute-start(bf16[128,2688]{1,0:T(8,128)(2,1)S(1)} %get-tuple-element.22), channel_id=1, source_target_pairs={{0,96},{32,0},{64,32},{96,64},{1,97},{33,1},{65,33},{97,65},{2,98}... | collective-permute-start | bytes 2064392 | tf_op jit(solution)/shard_map/ppermute | solution.py:19
  95.3 10.0 %collective-permute-start.18 = (bf16[256,2688]{1,0:T(8,128)(2,1)}, bf16[256,2688]{1,0:T(8,128)(2,1)S(1)}, u32[]{:S(2)}, u32[]{:S(2)}) collective-permute-start(bf16[256,2688]{1,0:T(8,128)(2,1)} %collective-permute-done.15.before.refs_2_), channel_id=1, source_target_pairs={{0,16},{16,0},{1,17},{17,1},{2,18},{18,2},{3,19},{19,3},{4,20},{20... | collective-permute-start | bytes 4128776 | tf_op jit(solution)/shard_map/ppermute | solution.py:440
  105.3 8.4 %collective-permute-start.21 = (bf16[128,2688]{1,0:T(8,128)(2,1)S(1)}, bf16[128,2688]{1,0:T(8,128)(2,1)S(1)}, u32[]{:S(2)}, u32[]{:S(2)}) collective-permute-start(bf16[128,2688]{1,0:T(8,128)(2,1)S(1)} %collective-permute-done.19.refs_6_), channel_id=1, source_target_pairs={{0,16},{16,0},{1,17},{17,1},{2,18},{18,2},{3,19},{19,3},{4,20},{20... | collective-permute-start | bytes 2064392 | tf_op jit(solution)/shard_map/ppermute | solution.py:440
  113.7 9.4 %collective-permute-done.20.refs_7_ = bf16[128,2688]{1,0:T(8,128)(2,1)S(1)} collective-permute-done((bf16[128,2688]{1,0:T(8,128)(2,1)S(1)}, bf16[128,2688]{1,0:T(8,128)(2,1)S(1)}, u32[]{:S(2)}, u32[]{:S(2)}) %collective-permute-start.20) | collective-permute-done | bytes 688160 | tf_op jit(solution)/shard_map/ppermute | solution.py:19
  128.5 11.6 %weight_grads.1 = (bf16[512,896]{1,0:T(8,128)(2,1)}, bf16[512,896]{1,0:T(8,128)(2,1)}, bf16[896,512]{1,0:T(8,128)(2,1)}, bf16[16,128]{1,0:T(8,128)(2,1)}) custom-call(s32[4]{0:T(128)} %copy-done.7, bf16[256,2688]{1,0:T(8,128)(2,1)} %copy-done, bf16[256,2688]{1,0:T(8,128)(2,1)} %collective-permute-done.14.after.refs_1_, ...), custom_call_target="tpu_custom_call" | custom-call | flops 5637144576 | bytes 15204352 | tf_op jit(solution)/shard_map/weight_grads/pallas_call | solution.py:346
  (89 shorter events, 17.6 us)
Async XLA Ops:
  7.2 121.4 %all-gather.3.cloned.1.call-start = ((), (), s32[]{:S(2)}) async-start(), calls=%async_computation.1 | async-start | bytes 4456448 | tf_op jit(solution)/shard_map/all_gather | solution.py:431
  7.2 10.8 %collective-permute-start.9 = (bf16[1,256,256]{2,1,0:T(8,128)(2,1)}, bf16[1,256,256]{2,1,0:T(8,128)(2,1)S(1)}, u32[]{:S(2)}, u32[]{:S(2)}) collective-permute-start(bf16[1,256,256]{2,1,0:T(8,128)(2,1)} %bitcast.14), channel_id=1, source_target_pairs={{0,8},{4,12},{8,0},{12,4},{1,9},{5,13},{9,1},{13,5},{2,10},{6,14},... | collective-permute-start | bytes 393224 | tf_op jit(solution)/shard_map/ppermute | solution.py:19
  11.1 9.0 %collective-permute-start.8 = (bf16[1,256,256]{2,1,0:T(8,128)(2,1)}, bf16[1,256,256]{2,1,0:T(8,128)(2,1)S(1)}, u32[]{:S(2)}, u32[]{:S(2)}) collective-permute-start(bf16[1,256,256]{2,1,0:T(8,128)(2,1)} %bitcast.15), channel_id=1, source_target_pairs={{0,4},{4,8},{8,12},{12,0},{1,5},{5,9},{9,13},{13,1},{2,6},{6,10},{... | collective-permute-start | bytes 393224 | tf_op jit(solution)/shard_map/ppermute | solution.py:19
  11.5 8.6 %collective-permute-start.7 = (bf16[1,256,256]{2,1,0:T(8,128)(2,1)}, bf16[1,256,256]{2,1,0:T(8,128)(2,1)S(1)}, u32[]{:S(2)}, u32[]{:S(2)}) collective-permute-start(bf16[1,256,256]{2,1,0:T(8,128)(2,1)} %bitcast.16), channel_id=1, source_target_pairs={{0,12},{4,0},{8,4},{12,8},{1,13},{5,1},{9,5},{13,9},{2,14},{6,2},{... | collective-permute-start | bytes 393224 | tf_op jit(solution)/shard_map/ppermute | solution.py:19
  13.7 10.0 %collective-permute-start.2 = (bf16[1,256,256]{2,1,0:T(8,128)(2,1)}, bf16[1,256,256]{2,1,0:T(8,128)(2,1)S(1)}, u32[]{:S(2)}, u32[]{:S(2)}) collective-permute-start(bf16[1,256,256]{2,1,0:T(8,128)(2,1)} %bitcast.10), channel_id=1, source_target_pairs={{0,2},{1,3},{2,0},{3,1},{4,6},{5,7},{6,4},{7,5},{8,10},{9,11},{10,... | collective-permute-start | bytes 393224 | tf_op jit(solution)/shard_map/ppermute | solution.py:19
  17.3 6.4 %collective-permute-start.1 = (bf16[1,256,256]{2,1,0:T(8,128)(2,1)}, bf16[1,256,256]{2,1,0:T(8,128)(2,1)S(1)}, u32[]{:S(2)}, u32[]{:S(2)}) collective-permute-start(bf16[1,256,256]{2,1,0:T(8,128)(2,1)} %bitcast.11), channel_id=1, source_target_pairs={{0,1},{1,2},{2,3},{3,0},{4,5},{5,6},{6,7},{7,4},{8,9},{9,10},{10,1... | collective-permute-start | bytes 393224 | tf_op jit(solution)/shard_map/ppermute | solution.py:19
  21.0 18.6 %collective-permute-start.12 = (bf16[4,256,256]{2,1,0:T(8,128)(2,1)S(1)}, bf16[4,256,256]{2,1,0:T(8,128)(2,1)S(1)}, u32[]{:S(2)}, u32[]{:S(2)}) collective-permute-start(bf16[4,256,256]{2,1,0:T(8,128)(2,1)S(1)} %pad_maximum_fusion.1.dy), channel_id=1, source_target_pairs={{0,1},{1,2},{2,3},{3,0},{4,5},{5,6},{6,7},{7,4},{8,9},{9,10},{10,1... | collective-permute-start | bytes 1572872 | tf_op jit(solution)/shard_map/ppermute | solution.py:19
  21.1 20.0 %collective-permute-start.10 = (bf16[4,256,256]{2,1,0:T(8,128)(2,1)S(1)}, bf16[4,256,256]{2,1,0:T(8,128)(2,1)S(1)}, u32[]{:S(2)}, u32[]{:S(2)}) collective-permute-start(bf16[4,256,256]{2,1,0:T(8,128)(2,1)S(1)} %pad_maximum_fusion.1.dy), channel_id=1, source_target_pairs={{0,3},{1,0},{2,1},{3,2},{4,7},{5,4},{6,5},{7,6},{8,11},{9,8},{10,9... | collective-permute-start | bytes 1572872 | tf_op jit(solution)/shard_map/ppermute | solution.py:19
  24.7 17.8 %collective-permute-start.5 = (bf16[4,256,256]{2,1,0:T(8,128)(2,1)S(1)}, bf16[4,256,256]{2,1,0:T(8,128)(2,1)S(1)}, u32[]{:S(2)}, u32[]{:S(2)}) collective-permute-start(bf16[4,256,256]{2,1,0:T(8,128)(2,1)S(1)} %pad_maximum_fusion.x), channel_id=1, source_target_pairs={{0,4},{4,8},{8,12},{12,0},{1,5},{5,9},{9,13},{13,1},{2,6},{6,10},{... | collective-permute-start | bytes 1572872 | tf_op jit(solution)/shard_map/ppermute | solution.py:19
  25.3 19.4 %collective-permute-start.3 = (bf16[4,256,256]{2,1,0:T(8,128)(2,1)S(1)}, bf16[4,256,256]{2,1,0:T(8,128)(2,1)S(1)}, u32[]{:S(2)}, u32[]{:S(2)}) collective-permute-start(bf16[4,256,256]{2,1,0:T(8,128)(2,1)S(1)} %pad_maximum_fusion.x), channel_id=1, source_target_pairs={{0,12},{4,0},{8,4},{12,8},{1,13},{5,1},{9,5},{13,9},{2,14},{6,2},{... | collective-permute-start | bytes 1572872 | tf_op jit(solution)/shard_map/ppermute | solution.py:19
  28.2 27.2 %collective-permute-start.23 = (bf16[512,256]{1,0:T(8,128)(2,1)}, bf16[512,256]{1,0:T(8,128)(2,1)S(1)}, u32[]{:S(2)}, u32[]{:S(2)}) collective-permute-start(bf16[512,256]{1,0:T(8,128)(2,1)} %pad_maximum_fusion.2), channel_id=1, source_target_pairs={{0,0},{1,2},{2,16},{3,18},{4,32},{5,34},{6,48},{7,50},{8,64},{9,66... | collective-permute-start | bytes 786440 | tf_op jit(solution)/shard_map/ppermute | solution.py:430
  39.7 14.9 %collective-permute-start.13 = (bf16[4,128,256]{2,1,0:T(8,128)(2,1)S(1)}, bf16[4,128,256]{2,1,0:T(8,128)(2,1)S(1)}, u32[]{:S(2)}, u32[]{:S(2)}) collective-permute-start(bf16[4,128,256]{2,1,0:T(8,128)(2,1)S(1)} %slice.19), channel_id=1, source_target_pairs={{0,1},{1,2},{2,3},{3,0},{4,5},{5,6},{6,7},{7,4},{8,9},{9,10},{10,1... | collective-permute-start | bytes 786440 | tf_op jit(solution)/shard_map/ppermute | solution.py:19
  41.1 13.4 %collective-permute-start.11 = (bf16[4,128,256]{2,1,0:T(8,128)(2,1)S(1)}, bf16[4,128,256]{2,1,0:T(8,128)(2,1)S(1)}, u32[]{:S(2)}, u32[]{:S(2)}) collective-permute-start(bf16[4,128,256]{2,1,0:T(8,128)(2,1)S(1)} %slice.18), channel_id=1, source_target_pairs={{0,3},{1,0},{2,1},{3,2},{4,7},{5,4},{6,5},{7,6},{8,11},{9,8},{10,9... | collective-permute-start | bytes 786440 | tf_op jit(solution)/shard_map/ppermute | solution.py:19
  42.5 12.1 %collective-permute-start.6 = (bf16[4,128,256]{2,1,0:T(8,128)(2,1)S(1)}, bf16[4,128,256]{2,1,0:T(8,128)(2,1)S(1)}, u32[]{:S(2)}, u32[]{:S(2)}) collective-permute-start(bf16[4,128,256]{2,1,0:T(8,128)(2,1)S(1)} %slice.17), channel_id=1, source_target_pairs={{0,4},{4,8},{8,12},{12,0},{1,5},{5,9},{9,13},{13,1},{2,6},{6,10},{... | collective-permute-start | bytes 786440 | tf_op jit(solution)/shard_map/ppermute | solution.py:19
  44.7 9.8 %collective-permute-start.4 = (bf16[4,128,256]{2,1,0:T(8,128)(2,1)S(1)}, bf16[4,128,256]{2,1,0:T(8,128)(2,1)S(1)}, u32[]{:S(2)}, u32[]{:S(2)}) collective-permute-start(bf16[4,128,256]{2,1,0:T(8,128)(2,1)S(1)} %slice.16), channel_id=1, source_target_pairs={{0,12},{4,0},{8,4},{12,8},{1,13},{5,1},{9,5},{13,9},{2,14},{6,2},{... | collective-permute-start | bytes 786440 | tf_op jit(solution)/shard_map/ppermute | solution.py:19
  64.9 26.3 %collective-permute-start.15 = (bf16[256,2688]{1,0:T(8,128)(2,1)S(1)}, bf16[256,2688]{1,0:T(8,128)(2,1)}, u32[]{:S(2)}, u32[]{:S(2)}) collective-permute-start(bf16[256,2688]{1,0:T(8,128)(2,1)S(1)} %forward_last.1.act.refs_0_), channel_id=1, source_target_pairs={{0,32},{32,64},{64,96},{96,0},{1,33},{33,65},{65,97},{97,1},{2,34}... | collective-permute-start | bytes 4128776 | tf_op jit(solution)/shard_map/ppermute | solution.py:19
  65.0 26.3 %collective-permute-start.14 = (bf16[256,2688]{1,0:T(8,128)(2,1)S(1)}, bf16[256,2688]{1,0:T(8,128)(2,1)}, u32[]{:S(2)}, u32[]{:S(2)}) collective-permute-start(bf16[256,2688]{1,0:T(8,128)(2,1)S(1)} %forward_last.1.act.refs_0_), channel_id=1, source_target_pairs={{0,96},{32,0},{64,32},{96,64},{1,97},{33,1},{65,33},{97,65},{2,98}... | collective-permute-start | bytes 4128776 | tf_op jit(solution)/shard_map/ppermute | solution.py:19
  76.3 63.9 %all-to-all-start = ((bf16[16,256,256]{2,1,0:T(8,128)(2,1)}), bf16[16,256,256]{2,1,0:T(8,128)(2,1)S(1)}, u32[]{:S(2)}, u32[]{:S(2)}) async-start(bf16[16,256,256]{2,1,0:T(8,128)(2,1)} %backward.1.behind), calls=%async_computation | async-start | bytes 4194304 | tf_op jit(solution)/shard_map/all_to_all | solution.py:437
  83.0 41.4 %collective-permute-start.16 = (bf16[256,2688]{1,0:T(8,128)(2,1)S(1)}, bf16[256,2688]{1,0:T(8,128)(2,1)S(1)}, u32[]{:S(2)}, u32[]{:S(2)}) collective-permute-start(bf16[256,2688]{1,0:T(8,128)(2,1)S(1)} %forward_last.1.act.refs_0_), channel_id=1, source_target_pairs={{0,16},{16,0},{1,17},{17,1},{2,18},{18,2},{3,19},{19,3},{4,20},{20... | collective-permute-start | bytes 4128776 | tf_op jit(solution)/shard_map/ppermute | solution.py:440
  92.6 12.7 %collective-permute-start.19 = (bf16[128,2688]{1,0:T(8,128)(2,1)S(1)}, bf16[128,2688]{1,0:T(8,128)(2,1)S(1)}, u32[]{:S(2)}, u32[]{:S(2)}) collective-permute-start(bf16[128,2688]{1,0:T(8,128)(2,1)S(1)} %get-tuple-element.22), channel_id=1, source_target_pairs={{0,96},{32,0},{64,32},{96,64},{1,97},{33,1},{65,33},{97,65},{2,98}... | collective-permute-start | bytes 2064392 | tf_op jit(solution)/shard_map/ppermute | solution.py:19
  95.3 30.2 %collective-permute-start.18 = (bf16[256,2688]{1,0:T(8,128)(2,1)}, bf16[256,2688]{1,0:T(8,128)(2,1)S(1)}, u32[]{:S(2)}, u32[]{:S(2)}) collective-permute-start(bf16[256,2688]{1,0:T(8,128)(2,1)} %collective-permute-done.15.before.refs_2_), channel_id=1, source_target_pairs={{0,16},{16,0},{1,17},{17,1},{2,18},{18,2},{3,19},{19,3},{4,20},{20... | collective-permute-start | bytes 4128776 | tf_op jit(solution)/shard_map/ppermute | solution.py:440
  105.3 21.3 %collective-permute-start.17 = (bf16[256,2688]{1,0:T(8,128)(2,1)}, bf16[256,2688]{1,0:T(8,128)(2,1)S(1)}, u32[]{:S(2)}, u32[]{:S(2)}) collective-permute-start(bf16[256,2688]{1,0:T(8,128)(2,1)} %collective-permute-done.14.after.refs_1_), channel_id=1, source_target_pairs={{0,16},{16,0},{1,17},{17,1},{2,18},{18,2},{3,19},{19,3},{4,20},{20... | collective-permute-start | bytes 4128776 | tf_op jit(solution)/shard_map/ppermute | solution.py:440
  105.3 17.8 %collective-permute-start.20 = (bf16[128,2688]{1,0:T(8,128)(2,1)S(1)}, bf16[128,2688]{1,0:T(8,128)(2,1)S(1)}, u32[]{:S(2)}, u32[]{:S(2)}) collective-permute-start(bf16[128,2688]{1,0:T(8,128)(2,1)S(1)} %get-tuple-element.23), channel_id=1, source_target_pairs={{0,32},{32,64},{64,96},{96,0},{1,33},{33,65},{65,97},{97,1},{2,34}... | collective-permute-start | bytes 2064392 | tf_op jit(solution)/shard_map/ppermute | solution.py:19
  105.3 22.4 %collective-permute-start.21 = (bf16[128,2688]{1,0:T(8,128)(2,1)S(1)}, bf16[128,2688]{1,0:T(8,128)(2,1)S(1)}, u32[]{:S(2)}, u32[]{:S(2)}) collective-permute-start(bf16[128,2688]{1,0:T(8,128)(2,1)S(1)} %collective-permute-done.19.refs_6_), channel_id=1, source_target_pairs={{0,16},{16,0},{1,17},{17,1},{2,18},{18,2},{3,19},{19,3},{4,20},{20... | collective-permute-start | bytes 2064392 | tf_op jit(solution)/shard_map/ppermute | solution.py:440
  (20 other events, 146.7 us)
Sparse Core Ops, SparseCore 0:
  56.6 71.2 all-gather.2

commit v4 on v3

--- a/solution.py
+++ b/solution.py
@@ -150,7 +150,7 @@
             pltpu.SemaphoreType.DMA((2,)),
         ]
         + group_buffers(depth, f_local, 1),
-        compiler_params=pltpu.CompilerParams(vmem_limit_bytes=48 * MIB),
+        compiler_params=pltpu.CompilerParams(vmem_limit_bytes=50 * MIB),
         cost_estimate=pl.CostEstimate(
             flops=24 * rows * depth * f_local,
             bytes_accessed=24 * depth * f_local,
@@ -227,7 +227,7 @@
             pltpu.SemaphoreType.DMA((2 * count + 3,)),
         ]
         + group_buffers(depth, f_local, count),
-        compiler_params=pltpu.CompilerParams(vmem_limit_bytes=48 * MIB),
+        compiler_params=pltpu.CompilerParams(vmem_limit_bytes=50 * MIB),
         cost_estimate=pl.CostEstimate(
             flops=24 * count * rows * depth * f_local,
             bytes_accessed=24 * count * depth * f_local,
@@ -286,7 +286,7 @@
     )(act, wg, wu)
 
 
-def weight_grads(coords, tiles, pieces):
+def weight_grads(coords, tiles, pieces, shares):
     count, chunks = len(tiles), (1, 3, 4)
     parts = [part for _, _, tile in tiles for part in tile]
     wide = parts[0].shape[1]
@@ -298,9 +298,8 @@
 
     def kernel(coords, *refs):
         acts, refs = list(refs[: len(parts)]), refs[len(parts) :]
-        pieces, outs, mark, accs, results = refs[0], refs[1:4], refs[4], refs[5:8], refs[8:11]
-        act_buf, tok_buf, cot_buf, sems = refs[11:]
-        mark[...] = jnp.zeros_like(mark)
+        pieces, shares, outs, accs, results = refs[0], refs[1], refs[2:6], refs[6:9], refs[9:13]
+        share_buf, act_buf, tok_buf, cot_buf, sems = refs[13:]
         x, c = coords[0], coords[1]
         used = [0]
 
@@ -323,6 +322,7 @@
                     target = buf.at[pl.ds(t * rows, rows), pl.ds(h * depth, depth)]
                     mine.append(start(pieces.at[piece, pl.ds(k * rows, rows)], target))
             loads.append(mine)
+        share_load = start(shares, share_buf)
         stores = []
         for t, chunk in zip((0, 1, 4), chunks):
             for load in sum(loads[t : t + chunk], []):
@@ -340,21 +340,28 @@
                 else:
                     results[k][...] = term.astype(results[k].dtype)
                     stores.append(start(results[k], outs[k]))
+        share_load.wait()
+        total = share_buf[0].astype(jnp.float32)
+        for k in range(1, shares.shape[0]):
+            total += share_buf[k].astype(jnp.float32)
+        results[3][...] = total.astype(results[3].dtype)
+        stores.append(start(results[3], outs[3]))
         for store in stores:
             store.wait()
 
-    return pl.pallas_call(
-        kernel,
-        in_specs=[IN_SMEM] + [ANYWHERE] * (len(parts) + 1),
-        out_specs=[ANYWHERE] * 3 + [IN_VMEM],
-        out_shape=[jax.ShapeDtypeStruct(shape, jnp.bfloat16) for shape in shapes + [(16, 128)]],
+    out_shapes = shapes + [shares.shape[1:]]
+    return pl.pallas_call(
+        kernel,
+        in_specs=[IN_SMEM] + [ANYWHERE] * (len(parts) + 2),
+        out_specs=[ANYWHERE] * 4,
+        out_shape=[jax.ShapeDtypeStruct(shape, jnp.bfloat16) for shape in out_shapes],
         scratch_shapes=[pltpu.VMEM(shape, jnp.float32) for shape in shapes]
-        + [pltpu.VMEM(shape, jnp.bfloat16) for shape in shapes]
+        + [pltpu.VMEM(shape, jnp.bfloat16) for shape in out_shapes + [shares.shape]]
         + [
             pltpu.VMEM((count * rows, wide), jnp.bfloat16),
             pltpu.VMEM((count * rows, cols), jnp.bfloat16),
             pltpu.VMEM((count * rows, cols), jnp.bfloat16),
-            pltpu.SemaphoreType.DMA((len(parts) + 4 * count + 3,)),
+            pltpu.SemaphoreType.DMA((len(parts) + 4 * count + 5,)),
         ],
         compiler_params=pltpu.CompilerParams(vmem_limit_bytes=58 * MIB),
         cost_estimate=pl.CostEstimate(
@@ -363,29 +370,7 @@
             transcendentals=0,
         ),
         name="weight_grads",
-    )(coords, *parts, pieces)
-
-
-def sum_shares(shares, behind):
-    n, rows, cols = shares.shape
-
-    def kernel(shares, behind, out):
-        total = shares[0].astype(jnp.float32)
-        for k in range(1, n):
-            total += shares[k].astype(jnp.float32)
-        out[...] = total.astype(out.dtype)
-
-    return pl.pallas_call(
-        kernel,
-        in_specs=[IN_VMEM, ANYWHERE],
-        out_specs=IN_VMEM,
-        out_shape=jax.ShapeDtypeStruct((rows, cols), shares.dtype),
-        compiler_params=pltpu.CompilerParams(vmem_limit_bytes=8 * MIB),
-        cost_estimate=pl.CostEstimate(
-            flops=n * rows * cols, bytes_accessed=2 * n * rows * cols, transcendentals=0
-        ),
-        name="sum_shares",
-    )(shares, behind)
+    )(coords, *parts, pieces, shares)
 
 
 def to_columns():
@@ -441,8 +426,7 @@
     tiles = [(0, False, [act]), (1, False, [after]), (3, False, [before])]
     tiles += [(o, True, [swap(p) for p in tile]) for o, _, tile in tiles]
     tiles += [(2, False, far), (2, True, [swap(p) for p in far])]
-    *grads, mark = weight_grads(coords, tiles, pieces)
-    input_grad = sum_shares(shares, mark)
+    *grads, input_grad = weight_grads(coords, tiles, pieces, shares)
     return (input_grad, *grads)
 
 

time: 149 us -> 148 us (level)
  waiting for transfers between devices: 13.3 us -> 18.3 us
  local copies, waits for them, and re-layouts: 8.44 us -> 4.41 us
  starting transfers between devices: 69.2 us -> 66.3 us
    unnamed x38 -> x30, local copies, waits for them, and re-layouts: 8.33 us -> 4.3 us
    all_gather x1, waiting for transfers between devices: 0.01 us -> 2.46 us  [per_device(): lax.all_gather(relay(turned, tok_far, cot_far, sums[0]), ('y', 'z'))]
    ppermute x5, waiting for transfers between devices: 0.01 us -> 2.09 us  [per_device(): swap = lambda a: lax.ppermute(a, 'c', [(0, 1), (1, 0)])]
    pallas_call x2, Pallas kernels: 12.2 us -> 14 us  [forward_more(): pl.pallas_call(kernel, in_specs=[IN_SMEM] * (2 if last else 1) + [ANYWHER...]
    ppermute x5, starting transfers between devices: 24.1 us -> 22.4 us  [per_device(): swap = lambda a: lax.ppermute(a, 'c', [(0, 1), (1, 0)])]
    pallas_call x2 -> x1, Pallas kernels: 12.5 us -> 11 us  [weight_grads(): pl.pallas_call(kernel, in_specs=[IN_SMEM] + [ANYWHERE] * (len(parts) + 2)...]
  transfers between devices with their start and end apart: 26 -> 26, of which waited for: 2 -> 5; matrix products, arithmetic and copies ran while one was open for 2% -> 2% of each run, Pallas kernels for 26% -> 20%
where the time goes in v4:
time: 148 us
  starting transfers between devices  66.3 us (45%)
  Pallas kernels  40.6 us (27%)
  waiting for transfers between devices  18.3 us (12%)
  between operations  15 us (10%)
  local copies, waits for them, and re-layouts  4.41 us (3%)
  other arithmetic  2.94 us (2%)
    ppermute x18, starting transfers between devices, from_offset(): lax.ppermute(value, axis, [(i, (i - offset) % RING) for i in range(RING)])  31 us
    ppermute x5, starting transfers between devices, per_device(): swap = lambda a: lax.ppermute(a, 'c', [(0, 1), (1, 0)])  22.4 us
    pallas_call x2, Pallas kernels, forward_more(): pl.pallas_call(kernel, in_specs=[IN_SMEM] * (2 if last else 1) + [ANYWHER...  14 us
    ppermute x18, waiting for transfers between devices, from_offset(): lax.ppermute(value, axis, [(i, (i - offset) % RING) for i in range(RING)])  13.7 us
    pallas_call x1, Pallas kernels, weight_grads(): pl.pallas_call(kernel, in_specs=[IN_SMEM] + [ANYWHERE] * (len(parts) + 2)...  11 us
    pallas_call x1, Pallas kernels, backward(): pl.pallas_call(kernel, in_specs=[IN_VMEM] + [ANYWHERE] * 2, out_specs=IN_...  8.79 us
    ppermute x1, starting transfers between devices, per_device(): turned = lax.ppermute(both, ('x', 'c', 'y', 'z'), to_columns())  6.89 us
    all_to_all x1, starting transfers between devices, per_device(): shares = lax.all_to_all(partial_dx, ('y', 'z'), 0, 0)  5.96 us
  transfers between devices with their start and end apart: 26, of which 5 were waited for; matrix products, arithmetic and copies ran while one was open for 2% of the time, Pallas kernels for 20%

profile of v4, /device:TPU:1, one launch (start us, length us, event | category | flops | bytes accessed | tf_op | source)
XLA Modules:
  0.0 147.6 jit_solution(1090299515489066816)
XLA Ops:
  7.2 3.8 %collective-permute-start.9 = (bf16[1,256,256]{2,1,0:T(8,128)(2,1)}, bf16[1,256,256]{2,1,0:T(8,128)(2,1)S(1)}, u32[]{:S(2)}, u32[]{:S(2)}) collective-permute-start(bf16[1,256,256]{2,1,0:T(8,128)(2,1)} %bitcast.14), channel_id=1, source_target_pairs={{0,8},{4,12},{8,0},{12,4},{1,9},{5,13},{9,1},{13,5},{2,10},{6,14},... | collective-permute-start | bytes 393224 | tf_op jit(solution)/shard_map/ppermute | solution.py:19
  11.5 2.3 %collective-permute-start.7 = (bf16[1,256,256]{2,1,0:T(8,128)(2,1)}, bf16[1,256,256]{2,1,0:T(8,128)(2,1)S(1)}, u32[]{:S(2)}, u32[]{:S(2)}) collective-permute-start(bf16[1,256,256]{2,1,0:T(8,128)(2,1)} %bitcast.16), channel_id=1, source_target_pairs={{0,12},{4,0},{8,4},{12,8},{1,13},{5,1},{9,5},{13,9},{2,14},{6,2},{... | collective-permute-start | bytes 393224 | tf_op jit(solution)/shard_map/ppermute | solution.py:19
  13.7 3.6 %collective-permute-start.2 = (bf16[1,256,256]{2,1,0:T(8,128)(2,1)}, bf16[1,256,256]{2,1,0:T(8,128)(2,1)S(1)}, u32[]{:S(2)}, u32[]{:S(2)}) collective-permute-start(bf16[1,256,256]{2,1,0:T(8,128)(2,1)} %bitcast.10), channel_id=1, source_target_pairs={{0,2},{1,3},{2,0},{3,1},{4,6},{5,7},{6,4},{7,5},{8,10},{9,11},{10,... | collective-permute-start | bytes 393224 | tf_op jit(solution)/shard_map/ppermute | solution.py:19
  18.1 1.9 %collective-permute-start = (bf16[1,256,256]{2,1,0:T(8,128)(2,1)}, bf16[1,256,256]{2,1,0:T(8,128)(2,1)S(1)}, u32[]{:S(2)}, u32[]{:S(2)}) collective-permute-start(bf16[1,256,256]{2,1,0:T(8,128)(2,1)} %bitcast.12), channel_id=1, source_target_pairs={{0,3},{1,0},{2,1},{3,2},{4,7},{5,4},{6,5},{7,6},{8,11},{9,8},{10,9... | collective-permute-start | bytes 393224 | tf_op jit(solution)/shard_map/ppermute | solution.py:19
  21.1 2.7 %collective-permute-start.10 = (bf16[4,256,256]{2,1,0:T(8,128)(2,1)S(1)}, bf16[4,256,256]{2,1,0:T(8,128)(2,1)S(1)}, u32[]{:S(2)}, u32[]{:S(2)}) collective-permute-start(bf16[4,256,256]{2,1,0:T(8,128)(2,1)S(1)} %pad_maximum_fusion.1.dy), channel_id=1, source_target_pairs={{0,3},{1,0},{2,1},{3,2},{4,7},{5,4},{6,5},{7,6},{8,11},{9,8},{10,9... | collective-permute-start | bytes 1572872 | tf_op jit(solution)/shard_map/ppermute | solution.py:19
  25.3 2.2 %collective-permute-start.3 = (bf16[4,256,256]{2,1,0:T(8,128)(2,1)S(1)}, bf16[4,256,256]{2,1,0:T(8,128)(2,1)S(1)}, u32[]{:S(2)}, u32[]{:S(2)}) collective-permute-start(bf16[4,256,256]{2,1,0:T(8,128)(2,1)S(1)} %pad_maximum_fusion.x), channel_id=1, source_target_pairs={{0,12},{4,0},{8,4},{12,8},{1,13},{5,1},{9,5},{13,9},{2,14},{6,2},{... | collective-permute-start | bytes 1572872 | tf_op jit(solution)/shard_map/ppermute | solution.py:19
  28.2 6.9 %collective-permute-start.23 = (bf16[512,256]{1,0:T(8,128)(2,1)}, bf16[512,256]{1,0:T(8,128)(2,1)S(1)}, u32[]{:S(2)}, u32[]{:S(2)}) collective-permute-start(bf16[512,256]{1,0:T(8,128)(2,1)} %pad_maximum_fusion.2), channel_id=1, source_target_pairs={{0,0},{1,2},{2,16},{3,18},{4,32},{5,34},{6,48},{7,50},{8,64},{9,66... | collective-permute-start | bytes 786440 | tf_op jit(solution)/shard_map/ppermute | solution.py:415
  35.2 4.4 %forward_first.1 = (f32[256,896]{1,0:T(8,128)S(1)}, f32[256,896]{1,0:T(8,128)S(1)}, f32[256,896]{1,0:T(8,128)S(1)}) custom-call(s32[4]{0:T(128)S(1)} %pad_add_fusion.coords, bf16[4,256,256]{2,1,0:T(8,128)(2,1)S(1)} %pad_maximum_fusion.x, bf16[4,256,256]{2,1,0:T(8,128)(2,1)S(1)} %pad_maximum_fusion.1.dy, bf16[4096,896]{1,0:T(8,128)(2,1)} %wg.3, ...), custom_call_target="tpu_custom_call" | custom-call | flops 1409286144 | bytes 5505024 | tf_op jit(solution)/shard_map/forward_first/pallas_call | solution.py:143
  43.4 2.2 %collective-permute-start.6 = (bf16[4,128,256]{2,1,0:T(8,128)(2,1)S(1)}, bf16[4,128,256]{2,1,0:T(8,128)(2,1)S(1)}, u32[]{:S(2)}, u32[]{:S(2)}) collective-permute-start(bf16[4,128,256]{2,1,0:T(8,128)(2,1)S(1)} %slice.17), channel_id=1, source_target_pairs={{0,4},{4,8},{8,12},{12,0},{1,5},{5,9},{9,13},{13,1},{2,6},{6,10},{... | collective-permute-start | bytes 786440 | tf_op jit(solution)/shard_map/ppermute | solution.py:19
  45.6 2.8 %collective-permute-start.4 = (bf16[4,128,256]{2,1,0:T(8,128)(2,1)S(1)}, bf16[4,128,256]{2,1,0:T(8,128)(2,1)S(1)}, u32[]{:S(2)}, u32[]{:S(2)}) collective-permute-start(bf16[4,128,256]{2,1,0:T(8,128)(2,1)S(1)} %slice.16), channel_id=1, source_target_pairs={{0,12},{4,0},{8,4},{12,8},{1,13},{5,1},{9,5},{13,9},{2,14},{6,2},{... | collective-permute-start | bytes 786440 | tf_op jit(solution)/shard_map/ppermute | solution.py:19
  48.4 7.8 %forward_near.1 = (f32[256,896]{1,0:T(8,128)S(1)}, f32[256,896]{1,0:T(8,128)S(1)}, f32[256,896]{1,0:T(8,128)}) custom-call(s32[4]{0:T(128)S(1)} %pad_add_fusion.coords, bf16[4,256,256]{2,1,0:T(8,128)(2,1)S(1)} %collective-permute-done.3.refs_0_, bf16[4,256,256]{2,1,0:T(8,128)(2,1)S(1)} %collective-permute-done.5.refs_1_, ...), custom_call_target="tpu_custom_call" | custom-call | flops 2818572288 | bytes 11010048 | tf_op jit(solution)/shard_map/forward_near/pallas_call | solution.py:219
  59.9 6.2 %forward_last.1.act.refs_0_ = bf16[256,2688]{1,0:T(8,128)(2,1)} custom-call(s32[4]{0:T(128)S(1)} %pad_add_fusion.coords, s32[7]{0:T(128)S(1)} %convert_element_type.3.refs_0_, bf16[4,256,256]{2,1,0:T(8,128)(2,1)S(1)} %constant_dynamic-update-slice_fusion.refs_1_, bf16[4,256,256]{2,1,0:T(8,128)(2,1)S(1)} %constant_dynamic-update-slice_fusion.2.refs_2_, ...), custom_call_target="tpu_custom_call" | custom-call | flops 1409286144 | bytes 5505024 | tf_op jit(solution)/shard_map/forward_last/pallas_call | solution.py:219
  66.3 2.7 %collective-permute-start.14 = (bf16[256,2688]{1,0:T(8,128)(2,1)}, bf16[256,2688]{1,0:T(8,128)(2,1)}, u32[]{:S(2)}, u32[]{:S(2)}) collective-permute-start(bf16[256,2688]{1,0:T(8,128)(2,1)} %forward_last.1.act.refs_0_), channel_id=1, source_target_pairs={{0,96},{32,0},{64,32},{96,64},{1,97},{33,1},{65,33},{97,65},{2,98}... | collective-permute-start | bytes 4128776 | tf_op jit(solution)/shard_map/ppermute | solution.py:19
  70.3 8.8 %backward.1.behind = bf16[16,256,256]{2,1,0:T(8,128)(2,1)} custom-call(bf16[256,2688]{1,0:T(8,128)(2,1)S(1)} %copy-done, bf16[4096,896]{1,0:T(8,128)(2,1)} %wg.3, bf16[4096,896]{1,0:T(8,128)(2,1)} %wu.3), custom_call_target="tpu_custom_call" | custom-call | flops 3758096384 | bytes 14680064 | tf_op jit(solution)/shard_map/backward/pallas_call | solution.py:269
  79.1 6.0 %all-to-all-start = ((bf16[16,256,256]{2,1,0:T(8,128)(2,1)}), bf16[16,256,256]{2,1,0:T(8,128)(2,1)}, u32[]{:S(2)}, u32[]{:S(2)}) async-start(bf16[16,256,256]{2,1,0:T(8,128)(2,1)} %backward.1.behind), calls=%async_computation | async-start | bytes 4194304 | tf_op jit(solution)/shard_map/all_to_all | solution.py:422
  85.1 5.1 %collective-permute-start.16 = (bf16[256,2688]{1,0:T(8,128)(2,1)S(1)}, bf16[256,2688]{1,0:T(8,128)(2,1)}, u32[]{:S(2)}, u32[]{:S(2)}) collective-permute-start(bf16[256,2688]{1,0:T(8,128)(2,1)S(1)} %copy-done.1), channel_id=1, source_target_pairs={{0,16},{16,0},{1,17},{17,1},{2,18},{18,2},{3,19},{19,3},{4,20},{20... | collective-permute-start | bytes 4128776 | tf_op jit(solution)/shard_map/ppermute | solution.py:425
  90.1 3.4 %collective-permute-done.15.before.refs_2_ = bf16[256,2688]{1,0:T(8,128)(2,1)S(1)} collective-permute-done((bf16[256,2688]{1,0:T(8,128)(2,1)}, bf16[256,2688]{1,0:T(8,128)(2,1)S(1)}, u32[]{:S(2)}, u32[]{:S(2)}) %collective-permute-start.15) | collective-permute-done | bytes 1376288 | tf_op jit(solution)/shard_map/ppermute | solution.py:19
  95.1 2.3 %collective-permute-start.19 = (bf16[128,2688]{1,0:T(8,128)(2,1)S(1)}, bf16[128,2688]{1,0:T(8,128)(2,1)S(1)}, u32[]{:S(2)}, u32[]{:S(2)}) collective-permute-start(bf16[128,2688]{1,0:T(8,128)(2,1)S(1)} %get-tuple-element.22), channel_id=1, source_target_pairs={{0,96},{32,0},{64,32},{96,64},{1,97},{33,1},{65,33},{97,65},{2,98}... | collective-permute-start | bytes 2064392 | tf_op jit(solution)/shard_map/ppermute | solution.py:19
  97.4 8.5 %collective-permute-start.18 = (bf16[256,2688]{1,0:T(8,128)(2,1)S(1)}, bf16[256,2688]{1,0:T(8,128)(2,1)}, u32[]{:S(2)}, u32[]{:S(2)}) collective-permute-start(bf16[256,2688]{1,0:T(8,128)(2,1)S(1)} %collective-permute-done.15.before.refs_2_), channel_id=1, source_target_pairs={{0,16},{16,0},{1,17},{17,1},{2,18},{18,2},{3,19},{19,3},{4,20},{20... | collective-permute-start | bytes 4128776 | tf_op jit(solution)/shard_map/ppermute | solution.py:425
  106.9 7.5 %collective-permute-start.21 = (bf16[128,2688]{1,0:T(8,128)(2,1)S(1)}, bf16[128,2688]{1,0:T(8,128)(2,1)}, u32[]{:S(2)}, u32[]{:S(2)}) collective-permute-start(bf16[128,2688]{1,0:T(8,128)(2,1)S(1)} %collective-permute-done.19.refs_6_), channel_id=1, source_target_pairs={{0,16},{16,0},{1,17},{17,1},{2,18},{18,2},{3,19},{19,3},{4,20},{20... | collective-permute-start | bytes 2064392 | tf_op jit(solution)/shard_map/ppermute | solution.py:425
  114.4 9.4 %collective-permute-done.20.refs_7_ = bf16[128,2688]{1,0:T(8,128)(2,1)} collective-permute-done((bf16[128,2688]{1,0:T(8,128)(2,1)S(1)}, bf16[128,2688]{1,0:T(8,128)(2,1)}, u32[]{:S(2)}, u32[]{:S(2)}) %collective-permute-start.20) | collective-permute-done | bytes 688160 | tf_op jit(solution)/shard_map/ppermute | solution.py:19
  125.1 2.1 %collective-permute-done.22.refs_9_ = bf16[128,2688]{1,0:T(8,128)(2,1)} collective-permute-done((bf16[128,2688]{1,0:T(8,128)(2,1)}, bf16[128,2688]{1,0:T(8,128)(2,1)}, u32[]{:S(2)}, u32[]{:S(2)}) %collective-permute-start.22) | collective-permute-done | bytes 688160 | tf_op jit(solution)/shard_map/ppermute | solution.py:425
  127.2 2.5 %all-gather.3.cloned.1.call-done = bf16[8192,256]{1,0:T(8,128)(2,1)} async-done(((bf16[512,256]{1,0:T(8,128)(2,1)}), bf16[8192,256]{1,0:T(8,128)(2,1)}) %all-gather.3.cloned.1.call-update) | async-done | bytes 4194320 | tf_op jit(solution)/shard_map/all_gather | solution.py:416
  129.7 11.0 %weight_grads.1 = (bf16[512,896]{1,0:T(8,128)(2,1)}, bf16[512,896]{1,0:T(8,128)(2,1)}, bf16[896,512]{1,0:T(8,128)(2,1)}, bf16[256,256]{1,0:T(8,128)(2,1)}) custom-call(s32[4]{0:T(128)} %copy-done.9, bf16[256,2688]{1,0:T(8,128)(2,1)} %forward_last.1.act.refs_0_, bf16[256,2688]{1,0:T(8,128)(2,1)} %collective-permute-done.14.after.refs_1_, ...), custom_call_target="tpu_custom_call" | custom-call | flops 5637144576 | bytes 15204352 | tf_op jit(solution)/shard_map/weight_grads/pallas_call | solution.py:353
  (80 shorter events, 16.8 us)
Async XLA Ops:
  7.2 122.5 %all-gather.3.cloned.1.call-start = ((), (), s32[]{:S(2)}) async-start(), calls=%async_computation.1 | async-start | bytes 4456448 | tf_op jit(solution)/shard_map/all_gather | solution.py:416
  7.2 10.8 %collective-permute-start.9 = (bf16[1,256,256]{2,1,0:T(8,128)(2,1)}, bf16[1,256,256]{2,1,0:T(8,128)(2,1)S(1)}, u32[]{:S(2)}, u32[]{:S(2)}) collective-permute-start(bf16[1,256,256]{2,1,0:T(8,128)(2,1)} %bitcast.14), channel_id=1, source_target_pairs={{0,8},{4,12},{8,0},{12,4},{1,9},{5,13},{9,1},{13,5},{2,10},{6,14},... | collective-permute-start | bytes 393224 | tf_op jit(solution)/shard_map/ppermute | solution.py:19
  11.1 9.0 %collective-permute-start.8 = (bf16[1,256,256]{2,1,0:T(8,128)(2,1)}, bf16[1,256,256]{2,1,0:T(8,128)(2,1)S(1)}, u32[]{:S(2)}, u32[]{:S(2)}) collective-permute-start(bf16[1,256,256]{2,1,0:T(8,128)(2,1)} %bitcast.15), channel_id=1, source_target_pairs={{0,4},{4,8},{8,12},{12,0},{1,5},{5,9},{9,13},{13,1},{2,6},{6,10},{... | collective-permute-start | bytes 393224 | tf_op jit(solution)/shard_map/ppermute | solution.py:19
  11.5 8.6 %collective-permute-start.7 = (bf16[1,256,256]{2,1,0:T(8,128)(2,1)}, bf16[1,256,256]{2,1,0:T(8,128)(2,1)S(1)}, u32[]{:S(2)}, u32[]{:S(2)}) collective-permute-start(bf16[1,256,256]{2,1,0:T(8,128)(2,1)} %bitcast.16), channel_id=1, source_target_pairs={{0,12},{4,0},{8,4},{12,8},{1,13},{5,1},{9,5},{13,9},{2,14},{6,2},{... | collective-permute-start | bytes 393224 | tf_op jit(solution)/shard_map/ppermute | solution.py:19
  13.7 10.0 %collective-permute-start.2 = (bf16[1,256,256]{2,1,0:T(8,128)(2,1)}, bf16[1,256,256]{2,1,0:T(8,128)(2,1)S(1)}, u32[]{:S(2)}, u32[]{:S(2)}) collective-permute-start(bf16[1,256,256]{2,1,0:T(8,128)(2,1)} %bitcast.10), channel_id=1, source_target_pairs={{0,2},{1,3},{2,0},{3,1},{4,6},{5,7},{6,4},{7,5},{8,10},{9,11},{10,... | collective-permute-start | bytes 393224 | tf_op jit(solution)/shard_map/ppermute | solution.py:19
  17.3 6.4 %collective-permute-start.1 = (bf16[1,256,256]{2,1,0:T(8,128)(2,1)}, bf16[1,256,256]{2,1,0:T(8,128)(2,1)S(1)}, u32[]{:S(2)}, u32[]{:S(2)}) collective-permute-start(bf16[1,256,256]{2,1,0:T(8,128)(2,1)} %bitcast.11), channel_id=1, source_target_pairs={{0,1},{1,2},{2,3},{3,0},{4,5},{5,6},{6,7},{7,4},{8,9},{9,10},{10,1... | collective-permute-start | bytes 393224 | tf_op jit(solution)/shard_map/ppermute | solution.py:19
  21.0 19.5 %collective-permute-start.12 = (bf16[4,256,256]{2,1,0:T(8,128)(2,1)S(1)}, bf16[4,256,256]{2,1,0:T(8,128)(2,1)S(1)}, u32[]{:S(2)}, u32[]{:S(2)}) collective-permute-start(bf16[4,256,256]{2,1,0:T(8,128)(2,1)S(1)} %pad_maximum_fusion.1.dy), channel_id=1, source_target_pairs={{0,1},{1,2},{2,3},{3,0},{4,5},{5,6},{6,7},{7,4},{8,9},{9,10},{10,1... | collective-permute-start | bytes 1572872 | tf_op jit(solution)/shard_map/ppermute | solution.py:19
  21.1 20.9 %collective-permute-start.10 = (bf16[4,256,256]{2,1,0:T(8,128)(2,1)S(1)}, bf16[4,256,256]{2,1,0:T(8,128)(2,1)S(1)}, u32[]{:S(2)}, u32[]{:S(2)}) collective-permute-start(bf16[4,256,256]{2,1,0:T(8,128)(2,1)S(1)} %pad_maximum_fusion.1.dy), channel_id=1, source_target_pairs={{0,3},{1,0},{2,1},{3,2},{4,7},{5,4},{6,5},{7,6},{8,11},{9,8},{10,9... | collective-permute-start | bytes 1572872 | tf_op jit(solution)/shard_map/ppermute | solution.py:19
  24.7 18.6 %collective-permute-start.5 = (bf16[4,256,256]{2,1,0:T(8,128)(2,1)S(1)}, bf16[4,256,256]{2,1,0:T(8,128)(2,1)S(1)}, u32[]{:S(2)}, u32[]{:S(2)}) collective-permute-start(bf16[4,256,256]{2,1,0:T(8,128)(2,1)S(1)} %pad_maximum_fusion.x), channel_id=1, source_target_pairs={{0,4},{4,8},{8,12},{12,0},{1,5},{5,9},{9,13},{13,1},{2,6},{6,10},{... | collective-permute-start | bytes 1572872 | tf_op jit(solution)/shard_map/ppermute | solution.py:19
  25.3 20.3 %collective-permute-start.3 = (bf16[4,256,256]{2,1,0:T(8,128)(2,1)S(1)}, bf16[4,256,256]{2,1,0:T(8,128)(2,1)S(1)}, u32[]{:S(2)}, u32[]{:S(2)}) collective-permute-start(bf16[4,256,256]{2,1,0:T(8,128)(2,1)S(1)} %pad_maximum_fusion.x), channel_id=1, source_target_pairs={{0,12},{4,0},{8,4},{12,8},{1,13},{5,1},{9,5},{13,9},{2,14},{6,2},{... | collective-permute-start | bytes 1572872 | tf_op jit(solution)/shard_map/ppermute | solution.py:19
  28.2 28.9 %collective-permute-start.23 = (bf16[512,256]{1,0:T(8,128)(2,1)}, bf16[512,256]{1,0:T(8,128)(2,1)S(1)}, u32[]{:S(2)}, u32[]{:S(2)}) collective-permute-start(bf16[512,256]{1,0:T(8,128)(2,1)} %pad_maximum_fusion.2), channel_id=1, source_target_pairs={{0,0},{1,2},{2,16},{3,18},{4,32},{5,34},{6,48},{7,50},{8,64},{9,66... | collective-permute-start | bytes 786440 | tf_op jit(solution)/shard_map/ppermute | solution.py:415
  40.5 15.7 %collective-permute-start.13 = (bf16[4,128,256]{2,1,0:T(8,128)(2,1)S(1)}, bf16[4,128,256]{2,1,0:T(8,128)(2,1)S(1)}, u32[]{:S(2)}, u32[]{:S(2)}) collective-permute-start(bf16[4,128,256]{2,1,0:T(8,128)(2,1)S(1)} %slice.19), channel_id=1, source_target_pairs={{0,1},{1,2},{2,3},{3,0},{4,5},{5,6},{6,7},{7,4},{8,9},{9,10},{10,1... | collective-permute-start | bytes 786440 | tf_op jit(solution)/shard_map/ppermute | solution.py:19
  42.0 14.2 %collective-permute-start.11 = (bf16[4,128,256]{2,1,0:T(8,128)(2,1)S(1)}, bf16[4,128,256]{2,1,0:T(8,128)(2,1)S(1)}, u32[]{:S(2)}, u32[]{:S(2)}) collective-permute-start(bf16[4,128,256]{2,1,0:T(8,128)(2,1)S(1)} %slice.18), channel_id=1, source_target_pairs={{0,3},{1,0},{2,1},{3,2},{4,7},{5,4},{6,5},{7,6},{8,11},{9,8},{10,9... | collective-permute-start | bytes 786440 | tf_op jit(solution)/shard_map/ppermute | solution.py:19
  43.4 12.9 %collective-permute-start.6 = (bf16[4,128,256]{2,1,0:T(8,128)(2,1)S(1)}, bf16[4,128,256]{2,1,0:T(8,128)(2,1)S(1)}, u32[]{:S(2)}, u32[]{:S(2)}) collective-permute-start(bf16[4,128,256]{2,1,0:T(8,128)(2,1)S(1)} %slice.17), channel_id=1, source_target_pairs={{0,4},{4,8},{8,12},{12,0},{1,5},{5,9},{9,13},{13,1},{2,6},{6,10},{... | collective-permute-start | bytes 786440 | tf_op jit(solution)/shard_map/ppermute | solution.py:19
  45.6 10.6 %collective-permute-start.4 = (bf16[4,128,256]{2,1,0:T(8,128)(2,1)S(1)}, bf16[4,128,256]{2,1,0:T(8,128)(2,1)S(1)}, u32[]{:S(2)}, u32[]{:S(2)}) collective-permute-start(bf16[4,128,256]{2,1,0:T(8,128)(2,1)S(1)} %slice.16), channel_id=1, source_target_pairs={{0,12},{4,0},{8,4},{12,8},{1,13},{5,1},{9,5},{13,9},{2,14},{6,2},{... | collective-permute-start | bytes 786440 | tf_op jit(solution)/shard_map/ppermute | solution.py:19
  66.2 27.3 %collective-permute-start.15 = (bf16[256,2688]{1,0:T(8,128)(2,1)}, bf16[256,2688]{1,0:T(8,128)(2,1)S(1)}, u32[]{:S(2)}, u32[]{:S(2)}) collective-permute-start(bf16[256,2688]{1,0:T(8,128)(2,1)} %forward_last.1.act.refs_0_), channel_id=1, source_target_pairs={{0,32},{32,64},{64,96},{96,0},{1,33},{33,65},{65,97},{97,1},{2,34}... | collective-permute-start | bytes 4128776 | tf_op jit(solution)/shard_map/ppermute | solution.py:19
  66.3 27.2 %collective-permute-start.14 = (bf16[256,2688]{1,0:T(8,128)(2,1)}, bf16[256,2688]{1,0:T(8,128)(2,1)}, u32[]{:S(2)}, u32[]{:S(2)}) collective-permute-start(bf16[256,2688]{1,0:T(8,128)(2,1)} %forward_last.1.act.refs_0_), channel_id=1, source_target_pairs={{0,96},{32,0},{64,32},{96,64},{1,97},{33,1},{65,33},{97,65},{2,98}... | collective-permute-start | bytes 4128776 | tf_op jit(solution)/shard_map/ppermute | solution.py:19
  79.1 46.0 %all-to-all-start = ((bf16[16,256,256]{2,1,0:T(8,128)(2,1)}), bf16[16,256,256]{2,1,0:T(8,128)(2,1)}, u32[]{:S(2)}, u32[]{:S(2)}) async-start(bf16[16,256,256]{2,1,0:T(8,128)(2,1)} %backward.1.behind), calls=%async_computation | async-start | bytes 4194304 | tf_op jit(solution)/shard_map/all_to_all | solution.py:422
  85.1 40.0 %collective-permute-start.16 = (bf16[256,2688]{1,0:T(8,128)(2,1)S(1)}, bf16[256,2688]{1,0:T(8,128)(2,1)}, u32[]{:S(2)}, u32[]{:S(2)}) collective-permute-start(bf16[256,2688]{1,0:T(8,128)(2,1)S(1)} %copy-done.1), channel_id=1, source_target_pairs={{0,16},{16,0},{1,17},{17,1},{2,18},{18,2},{3,19},{19,3},{4,20},{20... | collective-permute-start | bytes 4128776 | tf_op jit(solution)/shard_map/ppermute | solution.py:425
  95.1 11.8 %collective-permute-start.19 = (bf16[128,2688]{1,0:T(8,128)(2,1)S(1)}, bf16[128,2688]{1,0:T(8,128)(2,1)S(1)}, u32[]{:S(2)}, u32[]{:S(2)}) collective-permute-start(bf16[128,2688]{1,0:T(8,128)(2,1)S(1)} %get-tuple-element.22), channel_id=1, source_target_pairs={{0,96},{32,0},{64,32},{96,64},{1,97},{33,1},{65,33},{97,65},{2,98}... | collective-permute-start | bytes 2064392 | tf_op jit(solution)/shard_map/ppermute | solution.py:19
  97.4 27.7 %collective-permute-start.18 = (bf16[256,2688]{1,0:T(8,128)(2,1)S(1)}, bf16[256,2688]{1,0:T(8,128)(2,1)}, u32[]{:S(2)}, u32[]{:S(2)}) collective-permute-start(bf16[256,2688]{1,0:T(8,128)(2,1)S(1)} %collective-permute-done.15.before.refs_2_), channel_id=1, source_target_pairs={{0,16},{16,0},{1,17},{17,1},{2,18},{18,2},{3,19},{19,3},{4,20},{20... | collective-permute-start | bytes 4128776 | tf_op jit(solution)/shard_map/ppermute | solution.py:425
  105.9 19.2 %collective-permute-start.17 = (bf16[256,2688]{1,0:T(8,128)(2,1)}, bf16[256,2688]{1,0:T(8,128)(2,1)}, u32[]{:S(2)}, u32[]{:S(2)}) collective-permute-start(bf16[256,2688]{1,0:T(8,128)(2,1)} %collective-permute-done.14.after.refs_1_), channel_id=1, source_target_pairs={{0,16},{16,0},{1,17},{17,1},{2,18},{18,2},{3,19},{19,3},{4,20},{20... | collective-permute-start | bytes 4128776 | tf_op jit(solution)/shard_map/ppermute | solution.py:425
  105.9 17.8 %collective-permute-start.20 = (bf16[128,2688]{1,0:T(8,128)(2,1)S(1)}, bf16[128,2688]{1,0:T(8,128)(2,1)}, u32[]{:S(2)}, u32[]{:S(2)}) collective-permute-start(bf16[128,2688]{1,0:T(8,128)(2,1)S(1)} %get-tuple-element.23), channel_id=1, source_target_pairs={{0,32},{32,64},{64,96},{96,0},{1,33},{33,65},{65,97},{97,1},{2,34}... | collective-permute-start | bytes 2064392 | tf_op jit(solution)/shard_map/ppermute | solution.py:19
  106.9 18.2 %collective-permute-start.21 = (bf16[128,2688]{1,0:T(8,128)(2,1)S(1)}, bf16[128,2688]{1,0:T(8,128)(2,1)}, u32[]{:S(2)}, u32[]{:S(2)}) collective-permute-start(bf16[128,2688]{1,0:T(8,128)(2,1)S(1)} %collective-permute-done.19.refs_6_), channel_id=1, source_target_pairs={{0,16},{16,0},{1,17},{17,1},{2,18},{18,2},{3,19},{19,3},{4,20},{20... | collective-permute-start | bytes 2064392 | tf_op jit(solution)/shard_map/ppermute | solution.py:425
  (16 other events, 130.1 us)
Sparse Core Ops, SparseCore 0:
  58.0 71.6 all-gather.2
